TPU v7x, 32 devices: a whole 2x2x4 slice. The times are simulated.
32 devices in a mesh: lon: 8 (over y, x, core), rep: 4 (over z).
Axes of the slice: x: 2, y: 2, z: 4, core: 2. Of those that a mesh axis runs over, the one named last changes fastest.
Arguments:
- fields: bfloat16 [32, 24, 64, 256], P('rep', None, 'lon'), may hold values from -6 to 6
- stem_weight: bfloat16 [32, 24, 4, 4], replicated, may hold values from -0.3125 to 0.3125
- mid_weight: bfloat16 [64, 32, 3, 3], replicated, may hold values from -0.375 to 0.375
- head_weight: bfloat16 [64, 64, 3, 3], replicated, may hold values from -0.25 to 0.25
- out_weight: float32 [64], replicated, may hold values from -0.75 to 0.75
- pred_cotangent: float32 [32, 16, 64], P(('rep', 'lon')), may hold values from -6 to 6
Outputs:
- prediction: float32 [32, 16, 64], P(('rep', 'lon'))
- stem_cotangent: bfloat16 [32, 32, 32, 128], P('rep', None, 'lon')
- grad_stem: float32 [32, 24, 4, 4], replicated
- grad_mid: float32 [64, 32, 3, 3], replicated
- grad_head: float32 [64, 64, 3, 3], replicated
- grad_out: float32 [64], replicated
All inputs are finite; a program needn't handle non-finite values.
Results may differ from a plain program's by a relative error of at most 0.0085.
Values may be sent and summed in bfloat16 or wider, within the bound.
A program may use at most 128 MiB of HBM per device.

v0:
```python
import jax
import jax.numpy as jnp
from jax import lax
from jax.sharding import PartitionSpec as P


def extended_2(cells, sides, width):
    for axis, dim in sides:
        count = lax.axis_size(axis)
        head = lax.slice_in_dim(cells, 0, width, axis=dim)
        tail = lax.slice_in_dim(cells, cells.shape[dim] - width, cells.shape[dim], axis=dim)
        cells = jnp.concatenate(
            [
                lax.ppermute(tail, axis, [(i, (i + 1) % count) for i in range(count)]),
                cells,
                lax.ppermute(head, axis, [((i + 1) % count, i) for i in range(count)]),
            ],
            axis=dim,
        )
    return cells


def shifted(value, axis, steps):
    count = lax.axis_size(axis)
    pairs = [(source, (source + steps) % count) for source in range(count)]
    return lax.ppermute(value, axis, pairs)


def conv_forward(padded, weight, stride):
    return lax.conv_general_dilated(
        padded,
        weight,
        (stride, stride),
        "VALID",
        dimension_numbers=("NCHW", "OIHW", "NCHW"),
        preferred_element_type=jnp.float32,
    )


def conv_weight_grad(padded, cotangent, kernel, stride):
    out_rows, out_cols = (cotangent.shape[2], cotangent.shape[3])
    reach_rows = stride * (out_rows - 1) + kernel
    reach_cols = stride * (out_cols - 1) + kernel
    used = padded[:, :, :reach_rows, :reach_cols]
    return lax.conv_general_dilated(
        used,
        cotangent,
        (1, 1),
        "VALID",
        rhs_dilation=(stride, stride),
        dimension_numbers=("CNHW", "IOHW", "CNHW"),
        preferred_element_type=jnp.float32,
    )


def conv_input_grad(cotangent, weight, stride, padded_shape):
    kernel = weight.shape[2]
    out_rows, out_cols = (cotangent.shape[2], cotangent.shape[3])
    high_rows = padded_shape[2] - (stride * (out_rows - 1) + 1)
    high_cols = padded_shape[3] - (stride * (out_cols - 1) + 1)
    flipped = weight[:, :, ::-1, ::-1]
    return lax.conv_general_dilated(
        cotangent,
        flipped,
        (1, 1),
        ((kernel - 1, high_rows), (kernel - 1, high_cols)),
        lhs_dilation=(stride, stride),
        dimension_numbers=("NCHW", "IOHW", "NCHW"),
        preferred_element_type=jnp.float32,
    )


def slope(values):
    sigma = jax.nn.sigmoid(values)
    return sigma * (1.0 + values * (1.0 - sigma))


def lat_pad(field, before, after):
    return jnp.pad(field, ((0, 0), (0, 0), (0, 0), (before, after)))


def head_pass(mid_act, head_weight, out_weight, pred_cotangent):
    head_padded = lat_pad(
        jnp.concatenate([mid_act[:, :, -1:], mid_act, mid_act[:, :, :1]], 2), 1, 1
    )
    head_pre = conv_forward(head_padded, head_weight, 1)
    head_act = jax.nn.silu(head_pre).astype(jnp.bfloat16)
    head_wide = head_act.astype(jnp.float32)
    prediction = jnp.einsum("c,schw->shw", out_weight, head_wide)
    head_cot = (pred_cotangent[:, None] * out_weight[None, :, None, None] * slope(head_pre)).astype(
        jnp.bfloat16
    )
    out_sum = jnp.einsum("shw,schw->c", pred_cotangent, head_wide)
    head_sum = conv_weight_grad(head_padded, head_cot, 3, 1)
    head_spread = conv_input_grad(head_cot, head_weight, 1, head_padded.shape)
    mid_grad = head_spread[:, :, 1:-1, 1:-1]
    mid_grad = (
        mid_grad.at[:, :, -1]
        .add(head_spread[:, :, 0, 1:-1])
        .at[:, :, 0]
        .add(head_spread[:, :, -1, 1:-1])
    )
    return (prediction, mid_grad.astype(jnp.bfloat16), head_sum, out_sum)


def head_totals(head_sum, out_sum):
    return (head_sum, out_sum)


def local(fields, stem_weight, mid_weight, head_weight, out_weight, pred_cotangent):
    extended = extended_2(fields, (("lon", 2),), 1)
    padded_fields = lat_pad(extended, 1, 1)
    stem_pre = conv_forward(padded_fields, stem_weight, 2)
    stem_act = jax.nn.silu(stem_pre).astype(jnp.bfloat16)
    left_side = shifted(stem_act[:, :, -1:], "lon", 1)
    mid_padded = lat_pad(jnp.concatenate([left_side, stem_act], 2), 1, 0)
    mid_pre = conv_forward(mid_padded, mid_weight, 2)
    mid_act = jax.nn.silu(mid_pre).astype(jnp.bfloat16)
    mid_whole = lax.all_to_all(mid_act, "lon", split_axis=0, concat_axis=2, tiled=True)
    prediction, mid_whole_grad, head_sum, out_sum = head_pass(
        mid_whole, head_weight, out_weight, pred_cotangent
    )
    head_sum, out_sum = head_totals(head_sum, out_sum)
    mid_grad = lax.all_to_all(mid_whole_grad, "lon", split_axis=2, concat_axis=0, tiled=True)
    mid_cot = (mid_grad.astype(jnp.float32) * slope(mid_pre)).astype(jnp.bfloat16)
    mid_sum = conv_weight_grad(mid_padded, mid_cot, 3, 2)
    mid_spread = conv_input_grad(mid_cot, mid_weight, 2, mid_padded.shape)
    edge_part = shifted(mid_spread[:, :, 0:1, 1:].astype(jnp.bfloat16), "lon", -1).astype(
        jnp.float32
    )
    stem_grad = mid_spread[:, :, 1:, 1:].at[:, :, -1:].add(edge_part).astype(jnp.bfloat16)
    stem_cotangent = (stem_grad.astype(jnp.float32) * slope(stem_pre)).astype(jnp.bfloat16)
    stem_sum = conv_weight_grad(padded_fields, stem_cotangent, 4, 2)
    stem_sum, mid_sum, head_sum, out_sum = lax.psum(
        (stem_sum, mid_sum, head_sum, out_sum), ("lon", "rep")
    )
    factor = 1.0 / (fields.shape[0] * lax.axis_size("rep"))
    return (
        prediction,
        stem_cotangent,
        stem_sum * factor,
        mid_sum * factor,
        head_sum * factor,
        out_sum * factor,
    )


def solution(mesh):
    placed = (P("rep", None, "lon", None), P(), P(), P(), P(), P(("rep", "lon"), None, None))
    return jax.shard_map(
        local,
        mesh=mesh,
        in_specs=placed,
        out_specs=(P(("rep", "lon"), None, None), P("rep", None, "lon", None), P(), P(), P(), P()),
        check_vma=False,
    )
```

profile of v0, /device:TPU:0, one launch (start us, length us, event | category | flops | bytes accessed | tf_op | source)
XLA Modules:
  0.0 217.4 jit_solution(689651189464668795)
XLA Ops:
  7.2 5.0 %copy.79 = bf16[8,24,8,256]{1,0,3,2:T(8,128)(2,1)} copy(bf16[8,24,8,256]{3,2,1,0:T(8,128)(2,1)} %param.12) | data formatting | bytes 1572864 | tf_op args[0]
  12.2 1.3 fusion.40
  14.0 3.0 %collective-permute-start.1 = (bf16[8,24,1,256]{1,0,3,2:T(8,128)(2,1)S(1)}, bf16[8,24,1,256]{1,0,3,2:T(8,128)(2,1)S(1)}, u32[]{:S(2)}, u32[]{:S(2)}) collective-permute-start(bf16[8,24,1,256]{1,0,3,2:T(8,128)(2,1)S(1)} %get-tuple-element.71), channel_id=1, source_target_pairs={{4,0},{8,4},{12,8},{16,12},{20,16},{24,20},{28,24},{0,28},{5,1},{9... | collective-permute-start | bytes 294920 | tf_op jit(solution)/shard_map/ppermute | solution.py:16
  16.9 9.7 %collective-permute-done = bf16[8,24,1,256]{1,0,3,2:T(8,128)(2,1)S(1)} collective-permute-done((bf16[8,24,1,256]{1,0,3,2:T(8,128)(2,1)S(1)}, bf16[8,24,1,256]{1,0,3,2:T(8,128)(2,1)S(1)}, u32[]{:S(2)}, u32[]{:S(2)}) %collective-permute-start) | collective-permute-done | bytes 98336 | tf_op jit(solution)/shard_map/ppermute | solution.py:14
  26.7 1.5 collective-permute-done.1
  28.2 8.3 %multiply_convert_fusion.1 = (bf16[8,32,4,128]{1,0,3,2:T(8,128)(2,1)S(1)}, f32[8,32,4,128]{1,0,3,2:T(8,128)}) fusion(bf16[32,24,4,4]{0,3,2,1:T(4,128)(2,1)S(1)} %copy-done.13, bf16[8,24,1,256]{1,0,3,2:T(8,128)(2,1)S(1)} %collective-permute-done.1, bf16[8,24,8,256]{1,0,3,2:T(8,128)(2,1)} %copy.79, bf16[8,24,1,256]{1,0,3,2:T(8,128)(2,1)S(1)} %collective-permute-done), kind=kOutput, calls=%fused_computation.4 | convolution fusion | flops 103874560 | bytes 1794048 | tf_op jit(solution)/shard_map/conv_general_dilated | solution.py:30
  36.6 1.8 collective-permute-start.2
  38.4 5.1 %collective-permute-done.2 = bf16[8,32,1,128]{1,0,3,2:T(8,128)(2,1)S(1)} collective-permute-done((bf16[8,32,1,128]{1,0,3,2:T(8,128)(2,1)S(1)}, bf16[8,32,1,128]{1,0,3,2:T(8,128)(2,1)S(1)}, u32[]{:S(2)}, u32[]{:S(2)}) %collective-permute-start.2) | collective-permute-done | bytes 65568 | tf_op jit(solution)/shard_map/ppermute | solution.py:26
  43.5 0.9 multiply_convert_fusion.3
  44.5 0.9 reshape.166
  45.4 3.9 %all-to-all-start = ((bf16[8,2,4096]{2,1,0:T(2,128)(2,1)}), bf16[8,2,4096]{2,1,0:T(2,128)(2,1)S(1)}, u32[]{:S(2)}, u32[]{:S(2)}) async-start(bf16[8,2,4096]{2,1,0:T(2,128)(2,1)} %reshape.166), calls=%async_computation | async-start | bytes 262144 | tf_op jit(solution)/shard_map/all_to_all | solution.py:119
  49.4 5.4 %all-to-all-done = bf16[8,2,4096]{2,1,0:T(2,128)(2,1)S(1)} async-done(((bf16[8,2,4096]{2,1,0:T(2,128)(2,1)}), bf16[8,2,4096]{2,1,0:T(2,128)(2,1)S(1)}, u32[]{:S(2)}, u32[]{:S(2)}) %all-to-all-start) | async-done | bytes 131104 | tf_op jit(solution)/shard_map/all_to_all | solution.py:119
  55.7 1.1 pad_maximum_fusion.6
  57.7 1.0 add_multiply_fusion
  60.4 3.7 %fusion.10 = f32[64,64,3,3]{0,1,3,2:T(8,128)} fusion(bf16[1,64,18,64]{1,0,3,2:T(2,128)(2,1)S(1)} %pad_maximum_fusion.6, bf16[1,64,16,64]{1,2,3,0:T(8,128)(2,1)S(1)} %fusion.8), kind=kOutput, calls=%fused_computation.31 | convolution fusion | flops 74711040 | bytes 425984 | tf_op jit(solution)/shard_map/conv_general_dilated | solution.py:45
  64.5 0.7 fusion.42
  65.7 0.9 reshape.168
  66.6 3.4 %all-to-all-start.1 = ((bf16[8,2,4096]{2,1,0:T(2,128)(2,1)}), bf16[8,2,4096]{2,1,0:T(2,128)(2,1)S(1)}, u32[]{:S(2)}, u32[]{:S(2)}) async-start(bf16[8,2,4096]{2,1,0:T(2,128)(2,1)} %reshape.168), calls=%async_computation.1 | async-start | bytes 262144 | tf_op jit(solution)/shard_map/all_to_all | solution.py:124
  70.2 5.3 %all-to-all-done.1 = bf16[8,2,4096]{2,1,0:T(2,128)(2,1)S(1)} async-done(((bf16[8,2,4096]{2,1,0:T(2,128)(2,1)}), bf16[8,2,4096]{2,1,0:T(2,128)(2,1)S(1)}, u32[]{:S(2)}, u32[]{:S(2)}) %all-to-all-start.1) | async-done | bytes 131104 | tf_op jit(solution)/shard_map/all_to_all | solution.py:124
  76.3 1.4 fusion.45
  78.0 1.4 fusion.2
  79.5 1.1 slice.149
  80.6 1.3 collective-permute-done.3
  81.9 0.8 fusion.6
  82.6 2.6 %multiply_convert_fusion = bf16[8,32,4,128]{1,0,3,2:T(8,128)(2,1)S(1)} fusion(f32[8,32,4,128]{1,0,3,2:T(8,128)} %get-tuple-element.77, bf16[8,32,4,128]{1,0,3,2:T(8,128)(2,1)} %fusion.6), kind=kLoop, calls=%fused_computation.3 | loop fusion | flops 1310720 | bytes 1048576 | tf_op jit(solution)/shard_map/convert_element_type | solution.py:132
  85.3 4.5 %fusion = f32[32,24,4,4]{0,1,3,2:T(8,128)S(1)} fusion(bf16[8,32,4,128]{1,0,3,2:T(8,128)(2,1)S(1)} %multiply_convert_fusion, bf16[8,24,1,256]{1,0,3,2:T(8,128)(2,1)S(1)} %copy-done.10, bf16[8,24,8,256]{1,0,3,2:T(8,128)(2,1)S(1)} %copy-done.1, bf16[8,24,1,256]{1,0,3,2:T(8,128)(2,1)S(1)} %copy-done.8), kind=kOutput, calls=%fused_computation.1 | convolution fusion | flops 103219200 | bytes 1294336 | tf_op jit(solution)/shard_map/conv_general_dilated | solution.py:45
  89.8 43.6 %all-reduce = (f32[32,24,4,4]{0,1,3,2:T(8,128)S(1)}, f32[64]{0:T(128)S(1)}) all-reduce(f32[32,24,4,4]{0,1,3,2:T(8,128)S(1)} %fusion, f32[64]{0:T(128)S(1)} %convolution_bitcast_fusion), channel_id=1, replica_groups=mesh['lon'=8,'rep'=4] {'lon','rep'}, use_global_device_ids=true, to_apply=%region_0.1 | all-reduce | flops 12352 | bytes 98816 | tf_op jit(solution)/shard_map/psum | solution.py:134
  133.9 1.5 copy.104
  136.1 71.0 %all-reduce.4.cloned.1.call-done = (f32[64,32,3,3]{0,1,3,2:T(8,128)}, f32[64,64,3,3]{0,1,3,2:T(8,128)}) async-done(((f32[64,32,3,3]{0,1,3,2:T(8,128)}, f32[64,64,3,3]{0,1,3,2:T(8,128)}), (f32[64,32,3,3]{0,1,3,2:T(8,128)}, f32[64,64,3,3]{0,1,3,2:T(8,128)})) %all-reduce.4.cloned.1.call-update) | async-done | bytes 221200 | tf_op jit(solution)/shard_map/psum | solution.py:134
  207.1 1.6 broadcast_multiply_fusion.2
  208.7 1.0 broadcast_multiply_fusion
  209.7 0.9 copy.106
  (76 shorter events, 7.4 us)
Async XLA Ops:
  7.2 50.5 %copy-start = (bf16[64,64,3,3]{1,0,3,2:T(8,128)(2,1)S(1)}, bf16[64,64,3,3]{1,0,3,2:T(8,128)(2,1)}, u32[]{:S(2)}) copy-start(bf16[64,64,3,3]{1,0,3,2:T(8,128)(2,1)} %param.15) | copy-start | bytes 221188
  7.2 21.0 %copy-start.13 = (bf16[32,24,4,4]{0,3,2,1:T(4,128)(2,1)S(1)}, bf16[32,24,4,4]{0,3,2,1:T(4,128)(2,1)}, u32[]{:S(2)}) copy-start(bf16[32,24,4,4]{0,3,2,1:T(4,128)(2,1)} %param.13) | copy-start | bytes 73732
  13.5 13.2 %collective-permute-start = (bf16[8,24,1,256]{1,0,3,2:T(8,128)(2,1)S(1)}, bf16[8,24,1,256]{1,0,3,2:T(8,128)(2,1)S(1)}, u32[]{:S(2)}, u32[]{:S(2)}) collective-permute-start(bf16[8,24,1,256]{1,0,3,2:T(8,128)(2,1)S(1)} %get-tuple-element.70), channel_id=1, source_target_pairs={{0,4},{4,8},{8,12},{12,16},{16,20},{20,24},{24,28},{28,0},{1,5},{5... | collective-permute-start | bytes 294920 | tf_op jit(solution)/shard_map/ppermute | solution.py:14
  14.0 29.5 %copy-start.2 = (bf16[64,32,3,3]{0,1,3,2:T(8,128)(2,1)S(1)}, bf16[64,32,3,3]{0,1,3,2:T(8,128)(2,1)}, u32[]{:S(2)}) copy-start(bf16[64,32,3,3]{0,1,3,2:T(8,128)(2,1)} %param.14) | copy-start | bytes 110596
  14.0 14.2 %collective-permute-start.1 = (bf16[8,24,1,256]{1,0,3,2:T(8,128)(2,1)S(1)}, bf16[8,24,1,256]{1,0,3,2:T(8,128)(2,1)S(1)}, u32[]{:S(2)}, u32[]{:S(2)}) collective-permute-start(bf16[8,24,1,256]{1,0,3,2:T(8,128)(2,1)S(1)} %get-tuple-element.71), channel_id=1, source_target_pairs={{4,0},{8,4},{12,8},{16,12},{20,16},{24,20},{28,24},{0,28},{5,1},{9... | collective-permute-start | bytes 294920 | tf_op jit(solution)/shard_map/ppermute | solution.py:16
  26.7 9.9 %copy-start.7 = (bf16[8,24,1,256]{1,0,3,2:T(8,128)(2,1)}, bf16[8,24,1,256]{1,0,3,2:T(8,128)(2,1)S(1)}, u32[]{:S(2)}) copy-start(bf16[8,24,1,256]{1,0,3,2:T(8,128)(2,1)S(1)} %collective-permute-done) | copy-start | bytes 294916
  28.2 8.3 %copy-start.9 = (bf16[8,24,1,256]{1,0,3,2:T(8,128)(2,1)}, bf16[8,24,1,256]{1,0,3,2:T(8,128)(2,1)S(1)}, u32[]{:S(2)}) copy-start(bf16[8,24,1,256]{1,0,3,2:T(8,128)(2,1)S(1)} %collective-permute-done.1) | copy-start | bytes 294916
  36.5 7.9 %copy-start.3 = (bf16[8,32,4,128]{1,0,3,2:T(8,128)(2,1)}, bf16[8,32,4,128]{1,0,3,2:T(8,128)(2,1)S(1)}, u32[]{:S(2)}) copy-start(bf16[8,32,4,128]{1,0,3,2:T(8,128)(2,1)S(1)} %get-tuple-element.76) | copy-start | bytes 786436
  36.6 12.7 %copy-start.5 = (f32[1,16,64]{2,1,0:T(8,128)S(1)}, f32[1,16,64]{2,1,0:T(8,128)}, u32[]{:S(2)}) copy-start(f32[1,16,64]{2,1,0:T(8,128)} %param.17) | copy-start | bytes 12292
  36.6 6.9 %collective-permute-start.2 = (bf16[8,32,1,128]{1,0,3,2:T(8,128)(2,1)S(1)}, bf16[8,32,1,128]{1,0,3,2:T(8,128)(2,1)S(1)}, u32[]{:S(2)}, u32[]{:S(2)}) collective-permute-start(bf16[8,32,1,128]{1,0,3,2:T(8,128)(2,1)S(1)} %slice.136), channel_id=1, source_target_pairs={{0,4},{4,8},{8,12},{12,16},{16,20},{20,24},{24,28},{28,0},{1,5},{5... | collective-permute-start | bytes 196616 | tf_op jit(solution)/shard_map/ppermute | solution.py:26
  43.5 1.9 copy-start.11
  45.4 9.4 %all-to-all-start = ((bf16[8,2,4096]{2,1,0:T(2,128)(2,1)}), bf16[8,2,4096]{2,1,0:T(2,128)(2,1)S(1)}, u32[]{:S(2)}, u32[]{:S(2)}) async-start(bf16[8,2,4096]{2,1,0:T(2,128)(2,1)} %reshape.166), calls=%async_computation | async-start | bytes 262144 | tf_op jit(solution)/shard_map/all_to_all | solution.py:119
  55.2 2.4 %copy-start.15 = (pred[8,9]{0,1:T(8,128)(4,1)S(1)}, pred[8,9]{0,1:T(8,128)(4,1)}, u32[]{:S(2)}) copy-start(pred[8,9]{0,1:T(8,128)(4,1)} %constant.109) | copy-start | bytes 220
  57.7 1.1 copy-start.6
  58.7 0.7 copy-start.14
  66.6 8.8 %all-to-all-start.1 = ((bf16[8,2,4096]{2,1,0:T(2,128)(2,1)}), bf16[8,2,4096]{2,1,0:T(2,128)(2,1)S(1)}, u32[]{:S(2)}, u32[]{:S(2)}) async-start(bf16[8,2,4096]{2,1,0:T(2,128)(2,1)} %reshape.168), calls=%async_computation.1 | async-start | bytes 262144 | tf_op jit(solution)/shard_map/all_to_all | solution.py:124
  70.0 137.1 %all-reduce.4.cloned.1.call-start = ((), (), s32[]{:S(2)}) async-start(), calls=%async_computation.2 | async-start | bytes 884736 | tf_op jit(solution)/shard_map/psum | solution.py:134
  76.3 1.7 copy-start.4
  76.3 1.7 copy-start.12
  77.7 4.2 %collective-permute-start.3 = (bf16[8,32,1,128]{1,0,3,2:T(8,128)(2,1)S(1)}, bf16[8,32,1,128]{1,0,3,2:T(8,128)(2,1)S(1)}, u32[]{:S(2)}, u32[]{:S(2)}) collective-permute-start(bf16[8,32,1,128]{1,0,3,2:T(8,128)(2,1)S(1)} %slice.167), channel_id=1, source_target_pairs={{0,28},{4,0},{8,4},{12,8},{16,12},{20,16},{24,20},{28,24},{1,29},{... | collective-permute-start | bytes 196616 | tf_op jit(solution)/shard_map/ppermute | solution.py:26
  80.6 4.7 %copy-start.1 = (bf16[8,24,8,256]{1,0,3,2:T(8,128)(2,1)S(1)}, bf16[8,24,8,256]{1,0,3,2:T(8,128)(2,1)}, u32[]{:S(2)}) copy-start(bf16[8,24,8,256]{1,0,3,2:T(8,128)(2,1)} %copy.79) | copy-start | bytes 2359300
  80.6 4.7 %copy-start.8 = (bf16[8,24,1,256]{1,0,3,2:T(8,128)(2,1)S(1)}, bf16[8,24,1,256]{1,0,3,2:T(8,128)(2,1)}, u32[]{:S(2)}) copy-start(bf16[8,24,1,256]{1,0,3,2:T(8,128)(2,1)} %copy-done.7) | copy-start | bytes 294916
  80.6 4.7 %copy-start.10 = (bf16[8,24,1,256]{1,0,3,2:T(8,128)(2,1)S(1)}, bf16[8,24,1,256]{1,0,3,2:T(8,128)(2,1)}, u32[]{:S(2)}) copy-start(bf16[8,24,1,256]{1,0,3,2:T(8,128)(2,1)} %copy-done.9) | copy-start | bytes 294916
Sparse Core Ops, SparseCore 0:
  80.7 126.3 all-reduce.3
where the time goes:
time: 218 us; the launch traced here: 217 us
  waiting for transfers between devices  99.3 us (46%)
  blocking collectives  43.6 us (20%)
  matrix products  22.8 us (10%)
  local copies, waits for them, and re-layouts  15.9 us (7%)
  between operations  14.5 us (7%)
  starting transfers between devices  12.9 us (6%)
  other arithmetic  8.28 us (4%)
    psum x1, waiting for transfers between devices, local(): lax.psum((stem_sum, mid_sum, head_sum, out_sum), ('lon', 'rep'))  71 us
    psum x1, blocking collectives, local(): lax.psum((stem_sum, mid_sum, head_sum, out_sum), ('lon', 'rep'))  43.6 us
    unnamed x41, local copies, waits for them, and re-layouts  10.6 us
    conv_general_dilated x3, matrix products, conv_forward(): lax.conv_general_dilated(padded, weight, (stride, stride), 'VALID', dimen...  10.2 us
    ppermute x1, waiting for transfers between devices, extended_2(): lax.ppermute(tail, axis, [(i, (i + 1) % count) for i in range(count)])  9.74 us
    conv_general_dilated x3, matrix products, conv_weight_grad(): lax.conv_general_dilated(used, cotangent, (1, 1), 'VALID', rhs_dilation=(...  9.68 us
    ppermute x2, waiting for transfers between devices, shifted(): return lax.ppermute(value, axis, pairs)  6.37 us
    all_to_all x1, waiting for transfers between devices, local(): lax.all_to_all(mid_act, 'lon', split_axis=0, concat_axis=2, tiled=True)  5.44 us
  transfers between devices with their start and end apart: 7, of which 7 were waited for; matrix products, arithmetic and copies ran while one was open for 6% of the time, Pallas kernels for 0%

commit v1 on v0

v1 whole, which is shorter than its diff:
```python
import functools

import jax
import jax.numpy as jnp
from jax import lax
from jax.experimental import pallas as pl
from jax.experimental.pallas import tpu as pltpu
from jax.sharding import PartitionSpec as P

MESH = pl.DeviceIdType.MESH
F32 = jnp.float32
BF16 = jnp.bfloat16
C_IN, C_WIDE, C1, C2 = 24, 32, 32, 64


def grid_of(rows, cols):
    return (
        lax.broadcasted_iota(jnp.int32, (rows, cols), 0),
        lax.broadcasted_iota(jnp.int32, (rows, cols), 1),
    )


def ones_where(hit):
    return jnp.where(hit, 1.0, 0.0).astype(BF16)


def stem_pick():
    r, c = grid_of(256, 512)
    return ones_where(r == 2 * (c & 127) + (c >> 7) - 1)


def slab_order(width):
    r, c = grid_of(width * C_WIDE, C_IN * width)
    channel = r & (C_WIDE - 1)
    return ones_where((c == channel * width + (r >> 5)) & (channel < C_IN))


def mid_pick():
    r, c = grid_of(256, 384)
    return ones_where(((r >> 7) == ((c >> 6) & 1)) & ((r & 127) == 2 * (c & 63) + (c >> 7) - 1))


def mid_spread():
    r, c = grid_of(128, 768)
    return ones_where(
        ((r >> 6) == ((c >> 7) & 1)) & ((c & 127) == 2 * (r & 63) + (c >> 8) - 1)
    )


def dot(a, b, dims=((1,), (0,))):
    return lax.dot_general(a, b, (dims, ((), ())), preferred_element_type=F32)


def sigmoid(v):
    return 1.0 / (1.0 + jnp.exp(-v))


def slope_of(v, g):
    return g * (1.0 + v * (1.0 - g))


def swapped(tile):
    return pltpu.roll(tile, 64, axis=1)


def lon_shift(x, step):
    if step == 0:
        return x
    if step == 1:
        return jnp.concatenate([x[:, 128:], swapped(x[:, :128])], axis=1)
    return jnp.concatenate([swapped(x[:, -128:]), x[:, :-128]], axis=1)


def lat_shift(x, step):
    if step == 0:
        return x
    n = x.shape[1]
    lat = lax.broadcasted_iota(jnp.int32, x.shape, 1) & 63
    if step == 1:
        return jnp.where(lat == 63, 0.0, pltpu.roll(x, n - 1, axis=1))
    return jnp.where(lat == 0, 0.0, pltpu.roll(x, 1, axis=1))


def kernel(
    nl, nr, scen,
    fields, ws, wm, wmb, wh, ow, pc,
    pred, cot_out, g_stem, g_mid, g_head, g_out,
    got, e_buf, a_rows, f_buf, v_buf, m_rows, col_r, cc, cot_send,
    x_buf, half, got1, mine, got2, got3,
    own_sem, sf, rf, sc, rc, s1, r1, s2, r2, s3, r3,
):
    me, rep = lax.axis_index("lon"), lax.axis_index("rep")
    width = fields.shape[1] // C_IN
    per = width // 2
    lonh = nl * per
    hl = lonh // 2
    tiles = hl // 2

    def lon_peer(k):
        return (lax.rem(me + k, nl), rep)

    def rep_peer(k):
        return (me, lax.rem(rep + k, nr))

    def remote(src, dst, send, recv, peer):
        copy = pltpu.make_async_remote_copy(
            src_ref=src, dst_ref=dst, send_sem=send, recv_sem=recv,
            device_id=peer, device_id_type=MESH,
        )
        copy.start()
        return copy

    own = pltpu.make_async_copy(fields.at[me], got.at[me], own_sem.at[0])
    own.start()
    barrier = pltpu.get_barrier_semaphore()
    for k in range(1, nl):
        pl.semaphore_signal(barrier, inc=1, device_id=lon_peer(k), device_id_type=MESH)
    for k in range(1, nr):
        pl.semaphore_signal(barrier, inc=1, device_id=rep_peer(k), device_id_type=MESH)
    pl.semaphore_wait(barrier, nl - 1 + nr - 1)
    sends = []
    moved = []
    for k in range(1, nl):
        to = lax.rem(me + k, nl)
        moved.append(
            remote(fields.at[to], got.at[me], sf.at[k - 1], rf.at[k - 1], lon_peer(k))
        )
    sends += moved

    pick = stem_pick()
    order = slab_order(width)
    for k in range(nl):
        if k == 0:
            own.wait()
            source = me
        else:
            moved[k - 1].wait_recv()
            source = lax.rem(me - k + nl, nl)
        lines = dot(order, got[source]).astype(BF16)
        taps = dot(lines, pick).astype(BF16)
        for l in range(width):
            at = (l % 2 == 0)
            tile = source * per + l // 2 + (0 if at else 1)
            where = pl.ds(pl.multiple_of(tile * 128, 128), 128)
            for b in range(4):
                row = (128 if at else 0) + b * C_WIDE
                e_buf[row : row + C_WIDE, where] = taps[
                    l * C_WIDE : (l + 1) * C_WIDE, b * 128 : (b + 1) * 128
                ]
    e_buf[0:128, 0:128] = e_buf[0:128, lonh * 128 :]
    e_buf[128:256, lonh * 128 :] = e_buf[128:256, 0:128]

    both = dot(ws[...], e_buf[...])
    stem_pre = both[:C1, : lonh * 128] + both[C1:, 128:]
    stem_g = sigmoid(stem_pre)
    stem_act = (stem_pre * stem_g).astype(BF16)
    stem_slope = slope_of(stem_pre, stem_g)

    for l in range(hl):
        a_rows[l * C1 : (l + 1) * C1, 0:128] = stem_act[:, l * 128 : (l + 1) * 128]
        a_rows[l * C1 : (l + 1) * C1, 128:256] = stem_act[:, (l + hl) * 128 : (l + hl + 1) * 128]
    u = dot(a_rows[...], mid_pick())
    ub = u.astype(BF16)
    for b in range(3):
        last = u[(hl - 1) * C1 : hl * C1, b * 128 : (b + 1) * 128]
        f_buf[b * C1 : (b + 1) * C1, 0:128] = swapped(last).astype(BF16)
        for l in range(hl):
            t = (l + 1) // 2
            row = (96 if l % 2 == 0 else 0) + b * C1
            f_buf[row : row + C1, t * 128 : (t + 1) * 128] = ub[
                l * C1 : (l + 1) * C1, b * 128 : (b + 1) * 128
            ]
    n = tiles * 128
    mid_pre = dot(wm[0:192, :], f_buf[:, 0:n], ((0,), (0,))) + dot(
        wm[192:288, :], f_buf[0:96, 128 : n + 128], ((0,), (0,))
    )
    mid_g = sigmoid(mid_pre)
    mid_act = (mid_pre * mid_g).astype(BF16)
    mid_slope = slope_of(mid_pre, mid_g)

    y = dot(wh[...], mid_act)
    head_pre = None
    for b in range(3):
        s = None
        for a in range(3):
            block = (a * 3 + b) * C2
            part = lon_shift(y[block : block + C2], a - 1)
            s = part if s is None else s + part
        s = lat_shift(s, b - 1)
        head_pre = s if head_pre is None else head_pre + s
    head_g = sigmoid(head_pre)
    head_act = (head_pre * head_g).astype(BF16).astype(F32)
    pred[...] = jnp.sum(head_act * ow[...], axis=0, keepdims=True)
    out_sum = jnp.sum(head_act * pc[...], axis=1, keepdims=True)
    head_cot = (pc[...] * ow[...] * slope_of(head_pre, head_g)).astype(BF16).astype(F32)
    for b in range(3):
        moved_lat = lat_shift(head_cot, 1 - b)
        for a in range(3):
            block = (a * 3 + b) * C2
            col_r[block : block + C2, :] = lon_shift(moved_lat, 1 - a).astype(BF16)
    head_sum = dot(col_r[...], mid_act, ((1,), (1,)))
    mid_grad = dot(wh[...], col_r[...], ((0,), (0,))).astype(BF16).astype(F32)
    mid_cot = (mid_grad * mid_slope).astype(BF16)

    mid_sum_01 = dot(f_buf[:, 0:n], mid_cot, ((1,), (1,)))
    mid_sum_2 = dot(f_buf[0:96, 128 : n + 128], mid_cot, ((1,), (1,)))
    for t in range(tiles):
        m_rows[t * C2 : (t + 1) * C2, :] = mid_cot[:, t * 128 : (t + 1) * 128]
    up = dot(m_rows[...], mid_spread()).astype(BF16)
    for t in range(tiles):
        for b in range(3):
            for q in range(2):
                lon = t + q * tiles
                v_buf[b * C2 : (b + 1) * C2, lon * 128 : (lon + 1) * 128] = up[
                    t * C2 : (t + 1) * C2, b * 256 + q * 128 : b * 256 + (q + 1) * 128
                ]
    d = dot(wmb[...], v_buf[...])
    cc[0:C1, lonh * 128 :] = jnp.zeros((C1, 128), BF16)
    cc[C1 : 2 * C1, 0:128] = jnp.zeros((C1, 128), BF16)
    for i in range(lonh):
        m = i // 2
        if i % 2 == 0:
            grad = d[C1 : 2 * C1, m * 128 : (m + 1) * 128]
        else:
            nxt = (m + 1) % (lonh // 2)
            grad = d[2 * C1 :, m * 128 : (m + 1) * 128] + d[:C1, nxt * 128 : (nxt + 1) * 128]
        cot = grad.astype(BF16).astype(F32) * stem_slope[:, i * 128 : (i + 1) * 128]
        cot = cot.astype(BF16)
        cc[0:C1, i * 128 : (i + 1) * 128] = cot
        cc[C1 : 2 * C1, (i + 1) * 128 : (i + 2) * 128] = cot
        cot_send[i // per, :, (i % per) * 128 : (i % per + 1) * 128] = cot
    back = []
    for k in range(1, nl):
        to = lax.rem(me + k, nl)
        back.append(
            remote(cot_send.at[to], cot_out.at[me], sc.at[k - 1], rc.at[k - 1], lon_peer(k))
        )
    sends += back
    own_back = pltpu.make_async_copy(cot_send.at[me], cot_out.at[me], own_sem.at[1])
    own_back.start()
    stem_sum = dot(e_buf[...], cc[...], ((1,), (1,)))

    total_rows = x_buf.shape[0]
    rows = total_rows // nl
    left = [head_sum, jnp.broadcast_to(out_sum, (C2, C2))]
    right = [mid_sum_01, mid_sum_2, stem_sum]
    if total_rows > 640:
        left.append(jnp.zeros((total_rows - 640, 64), F32))
    right.append(jnp.zeros((total_rows - 544, 64), F32))
    x = jnp.concatenate(
        [jnp.concatenate(left, axis=0), jnp.concatenate(right, axis=0)], axis=1
    )
    x_buf[...] = x
    half[...] = x.astype(BF16)

    def part_of(at):
        return pl.ds(pl.multiple_of(at * rows, 16), rows)

    first = []
    for k in range(1, nl):
        to = lax.rem(me + k, nl)
        first.append(
            remote(half.at[part_of(to)], got1.at[k - 1], s1.at[k - 1], r1.at[k - 1], lon_peer(k))
        )
    total = x_buf[part_of(me), :]
    for k in range(1, nl):
        first[k - 1].wait_recv()
        total = total + got1[k - 1].astype(F32)
    mine[...] = total.astype(BF16)
    second = []
    for k in range(1, nr):
        second.append(remote(mine, got2.at[rep], s2.at[k - 1], r2.at[k - 1], rep_peer(k)))
    got2[rep] = mine[...]
    for copy in second:
        copy.wait_recv()
    total = got2[0].astype(F32)
    for k in range(1, nr):
        total = total + got2[k].astype(F32)
    got3[part_of(me), :] = total.astype(BF16)
    third = []
    for k in range(1, nl):
        third.append(
            remote(
                got3.at[part_of(me)], got3.at[part_of(me)], s3.at[k - 1], r3.at[k - 1], lon_peer(k)
            )
        )
    for copy in third:
        copy.wait_recv()
    factor = 1.0 / scen
    summed = got3[...].astype(F32) * factor
    g_head[...] = summed[0:576, 0:64]
    g_out[...] = summed[576:640, 0:1]
    g_mid[...] = summed[0:288, 64:128]
    g_stem[...] = summed[288:544, 64:128]
    own_back.wait()
    for copy in back:
        copy.wait_recv()
    for copy in sends + first + second + third:
        copy.wait_send()


def local(nl, nr, fields, stem_weight, mid_weight, head_weight, out_weight, pred_cotangent):
    scen_here, _, width, lat = fields.shape
    per = width // 2
    lonh = nl * per
    tiles = lonh // 4
    lonc = 2 * tiles
    x_rows = -(-640 // (nl * 16)) * nl * 16
    rows = x_rows // nl
    ws = jnp.pad(stem_weight, ((0, 0), (0, C_WIDE - C_IN), (0, 0), (0, 0)))
    ws = ws.reshape(C1, C_WIDE, 2, 2, 4).transpose(2, 0, 3, 4, 1).reshape(2 * C1, 256)
    wm = mid_weight.transpose(2, 3, 1, 0).reshape(288, C2)
    wmb = mid_weight.transpose(2, 1, 3, 0).reshape(96, 192)
    wh = head_weight.transpose(2, 3, 0, 1).reshape(576, C2)
    pc = pred_cotangent.reshape(2, tiles, 64).transpose(1, 0, 2).reshape(1, tiles * 128)
    vmem = pl.BlockSpec(memory_space=pltpu.VMEM)
    hbm = pl.BlockSpec(memory_space=pl.ANY)
    dma = pltpu.SemaphoreType.DMA
    pred, cot, g_stem, g_mid, g_head, g_out = pl.pallas_call(
        functools.partial(kernel, nl, nr, scen_here * nr),
        out_shape=[
            jax.ShapeDtypeStruct((1, tiles * 128), F32),
            jax.ShapeDtypeStruct((nl, C1, per * 128), BF16),
            jax.ShapeDtypeStruct((256, C2), F32),
            jax.ShapeDtypeStruct((288, C2), F32),
            jax.ShapeDtypeStruct((576, C2), F32),
            jax.ShapeDtypeStruct((C2, 1), F32),
        ],
        in_specs=[hbm] + [vmem] * 6,
        out_specs=[vmem, hbm, vmem, vmem, vmem, vmem],
        scratch_shapes=[
            pltpu.VMEM((nl, C_IN * width, lat), BF16),
            pltpu.VMEM((256, (lonh + 1) * 128), BF16),
            pltpu.VMEM((lonh // 2 * C1, 256), BF16),
            pltpu.VMEM((192, (tiles + 1) * 128), BF16),
            pltpu.VMEM((192, lonc * 128), BF16),
            pltpu.VMEM((tiles * C2, 128), BF16),
            pltpu.VMEM((576, tiles * 128), BF16),
            pltpu.VMEM((2 * C1, (lonh + 1) * 128), BF16),
            pltpu.VMEM((nl, C1, per * 128), BF16),
            pltpu.VMEM((x_rows, 128), F32),
            pltpu.VMEM((x_rows, 128), BF16),
            pltpu.VMEM((nl - 1, rows, 128), BF16),
            pltpu.VMEM((rows, 128), BF16),
            pltpu.VMEM((nr, rows, 128), BF16),
            pltpu.VMEM((x_rows, 128), BF16),
            dma((2,)),
            dma((nl - 1,)), dma((nl - 1,)),
            dma((nl - 1,)), dma((nl - 1,)),
            dma((nl - 1,)), dma((nl - 1,)),
            dma((nr - 1,)), dma((nr - 1,)),
            dma((nl - 1,)), dma((nl - 1,)),
        ],
        compiler_params=pltpu.CompilerParams(
            collective_id=0, has_side_effects=True, vmem_limit_bytes=50 * 2**20
        ),
    )(
        fields.reshape(scen_here, C_IN * width, lat),
        ws, wm, wmb, wh, out_weight.reshape(C2, 1), pc,
    )
    prediction = pred.reshape(tiles, 2, 64).transpose(1, 0, 2).reshape(1, lonc, 64)
    stem_cotangent = cot.reshape(nl, C1, per, 128)
    grad_stem = g_stem.reshape(2, 4, C_WIDE, 2, C1)[:, :, :C_IN].transpose(4, 2, 3, 0, 1)
    grad_stem = grad_stem.reshape(C1, C_IN, 4, 4)
    grad_mid = g_mid.reshape(3, 3, C1, C2).transpose(3, 2, 0, 1)
    grad_head = g_head.reshape(3, 3, C2, C2).transpose(2, 3, 0, 1)
    return prediction, stem_cotangent, grad_stem, grad_mid, grad_head, g_out.reshape(C2)


def solution(mesh):
    placed = (P("rep", None, "lon", None), P(), P(), P(), P(), P(("rep", "lon"), None, None))
    return jax.shard_map(
        functools.partial(local, mesh.shape["lon"], mesh.shape["rep"]),
        mesh=mesh,
        in_specs=placed,
        out_specs=(P(("rep", "lon"), None, None), P("rep", None, "lon", None), P(), P(), P(), P()),
        check_vma=False,
    )
```

time: 218 us -> 44.8 us (0.21)
  waiting for transfers between devices: 99.3 us -> 0 us
  blocking collectives: 43.6 us -> 0 us
  Pallas kernels: 0 us -> 34.3 us
  matrix products: 22.8 us -> 0 us
  between operations: 14.5 us -> 0.72 us
  starting transfers between devices: 12.9 us -> 0 us
  local copies, waits for them, and re-layouts: 15.9 us -> 8.29 us
  other arithmetic: 8.28 us -> 1.29 us
    psum x1 -> x0, waiting for transfers between devices: 71 us -> none  [local(): lax.psum((stem_sum, mid_sum, head_sum, out_sum), ('lon', 'rep'))]
    psum x1 -> x0, blocking collectives: 43.6 us -> none  [local(): lax.psum((stem_sum, mid_sum, head_sum, out_sum), ('lon', 'rep'))]
    pallas_call x0 -> x1, Pallas kernels: none -> 34.3 us  [local(): pl.pallas_call(functools.partial(kernel, nl, nr, scen_here * nr), out_sha...]
    conv_general_dilated x8 -> x0, matrix products: 21.9 us -> none  [the longest x3 10.2 us: conv_forward(): lax.conv_general_dilated(padded, weight, (stride, stride), 'VALID', dimen...]
    ppermute x4 -> x0, waiting for transfers between devices: 17.6 us -> none  [the longest x1 9.74 us: extended_2(): lax.ppermute(tail, axis, [(i, (i + 1) % count) for i in range(count)])]
    all_to_all x2 -> x0, waiting for transfers between devices: 10.7 us -> none  [the longest x1 5.44 us: local(): lax.all_to_all(mid_act, 'lon', split_axis=0, concat_axis=2, tiled=True)]
    unnamed x41 -> x9, local copies, waits for them, and re-layouts: 10.6 us -> 2.89 us
    all_to_all x2 -> x0, starting transfers between devices: 7.29 us -> none  [the longest x1 3.92 us: local(): lax.all_to_all(mid_act, 'lon', split_axis=0, concat_axis=2, tiled=True)]
  transfers between devices with their start and end apart: 7 -> 0, of which waited for: 7 -> 0; matrix products, arithmetic and copies ran while one was open for 6% -> 0% of each run, Pallas kernels for 0% -> 0%
where the time goes in v1:
time: 44.8 us; the launch traced here: 44.6 us
  Pallas kernels  34.3 us (77%)
  local copies, waits for them, and re-layouts  8.29 us (19%)
  other arithmetic  1.29 us (3%)
  between operations  0.72 us (2%)
    pallas_call x1, Pallas kernels, local(): pl.pallas_call(functools.partial(kernel, nl, nr, scen_here * nr), out_sha...  34.3 us
    unnamed x9, local copies, waits for them, and re-layouts  2.89 us
    pallas_call x2, other arithmetic, local(): pl.pallas_call(functools.partial(kernel, nl, nr, scen_here * nr), out_sha...  1.29 us
    pad x1, local copies, waits for them, and re-layouts, local(): ws = jnp.pad(stem_weight, ((0, 0), (0, C_WIDE - C_IN), (0, 0), (0, 0)))  0.95 us

profile of v1, /device:TPU:0, one launch (start us, length us, event | category | flops | bytes accessed | tf_op | source)
XLA Modules:
  0.0 44.6 jit_solution(15371981773087930998)
XLA Ops:
  0.6 0.0 copy-start.1
  0.6 0.0 copy-start
  0.7 0.8 %copy.35 = f32[2,8,64]{2,0,1:T(2,128)S(1)} copy(f32[2,8,64]{2,1,0:T(8,128)} %bitcast.41) | data formatting | bytes 8192 | tf_op jit(solution)/shard_map/reshape | solution.py:315
  1.4 0.1 reshape.71.pc
  1.5 0.7 %copy.27.ow = f32[64,1]{1,0:T(8,128)S(1)} copy(f32[64,1]{0,1:T(1,128)} %bitcast.43) | data formatting | bytes 512 | tf_op jit(solution)/shard_map/reshape | solution.py:359
  2.3 0.0 copy-done.1
  2.3 0.1 copy.25
  2.3 0.1 reshape.67.wmb
  2.4 0.9 %pad.4 = bf16[32,32,4,4]{0,3,2,1:T(4,128)(2,1)S(1)} pad(bf16[32,24,4,4]{0,3,2,1:T(4,128)(2,1)} %param.7, bf16[]{:T(256)} %constant.2.clone.1), padding=0_0x0_8x0_0x0_0 | pad | bytes 57346 | tf_op jit(solution)/shard_map/jit(_pad)/pad | solution.py:310
  3.4 0.2 copy.24
  3.6 0.0 copy-start.2
  3.6 0.1 reshape.65.ws
  3.7 0.0 copy-done
  3.7 0.8 %copy-done.2 = bf16[64,64,3,3]{1,0,3,2:T(8,128)(2,1)S(1)} copy-done((bf16[64,64,3,3]{1,0,3,2:T(8,128)(2,1)S(1)}, bf16[64,64,3,3]{1,0,3,2:T(8,128)(2,1)}, u32[]{:S(2)}) %copy-start.2) | copy-done | bytes 73752
  4.5 34.3 %shard_map.109 = (f32[1,1024]{1,0:T(1,128)S(1)}, bf16[8,32,512]{2,1,0:T(8,128)(2,1)S(1)}, f32[256,64]{1,0:T(8,128)S(1)}, f32[288,64]{1,0:T(8,128)S(1)}, f32[576,64]{1,0:T(8,128)S(1)}, /*index=5*/f32[64,1]{1,0:T(8,128)S(1)}) custom-call(bf16[8,192,256]{2,1,0:T(8,128)(2,1)S(1)} %bitcast.30, bf16[64,256]{1,0:T(8,128)(2,1)S(1)} %reshape.65.ws, ...), custom_call_target="tpu_custom_call" | custom-call | tf_op jit(solution)/shard_map/pallas_call | solution.py:319
  38.8 0.5 %broadcast.6 = f32[]{:T(128)} broadcast(f32[]{:T(128)} %constant.7), dimensions={} | broadcast | bytes 8 | tf_op jit(solution)/shard_map/pallas_call | solution.py:319
  39.3 0.7 %reduce.4 = f32[1024]{0:T(1024)S(1)} reduce(f32[1,1024]{1,0:T(1,128)S(1)} %get-tuple-element.12, f32[]{:T(128)} %broadcast.6), dimensions={0}, to_apply=%get-tuple-element.12.reduce_sub_computation.3 | reduce | bytes 8196 | tf_op jit(solution)/shard_map/pallas_call | solution.py:319
  40.0 0.6 %reduce.1 = f32[64]{0:T(128)} reduce(f32[64,1]{1,0:T(8,128)S(1)} %get-tuple-element.17, f32[]{:T(128)} %constant.7), dimensions={1}, to_apply=%get-tuple-element.17.reduce_sub_computation | reduce | bytes 516 | tf_op jit(solution)/shard_map/pallas_call | solution.py:319
  40.6 0.1 reshape.72
  40.7 0.6 %copy.34 = f32[2,8,64]{2,1,0:T(8,128)} copy(f32[2,8,64]{2,0,1:T(2,128)S(1)} %bitcast.39) | data formatting | bytes 8192 | tf_op jit(solution)/shard_map/transpose | solution.py:361
  41.3 0.1 copy.29
  41.3 0.2 reshape.75
  41.5 0.1 copy.30
  41.7 0.7 %copy.31 = f32[32,24,4,4]{0,3,2,1:T(4,128)} copy(f32[32,24,4,4]{0,1,3,2:T(8,128)S(1)} %bitcast.36) | data formatting | bytes 98304
  42.4 0.8 %reshape.74 = bf16[8,32,4,128]{3,2,1,0:T(4,128)(2,1)} reshape(bf16[8,32,512]{2,1,0:T(8,128)(2,1)S(1)} %get-tuple-element.13) | data formatting | bytes 524288 | tf_op jit(solution)/shard_map/reshape | solution.py:362
  43.2 0.7 %copy.38 = f32[64,32,3,3]{0,1,3,2:T(8,128)} copy(f32[64,32,3,3]{0,1,3,2:T(8,128)S(1)} %bitcast.35) | data formatting | bytes 147456
  43.8 0.7 %copy.39 = f32[64,64,3,3]{1,0,3,2:T(8,128)} copy(f32[64,64,3,3]{1,0,3,2:T(8,128)S(1)} %bitcast.33) | data formatting | bytes 294912
  (1 shorter events, 0.0 us)
Async XLA Ops:
  0.6 1.6 %copy-start.1 = (bf16[64,32,3,3]{0,1,3,2:T(8,128)(2,1)S(1)}, bf16[64,32,3,3]{0,1,3,2:T(8,128)(2,1)}, u32[]{:S(2)}) copy-start(bf16[64,32,3,3]{0,1,3,2:T(8,128)(2,1)} %param.8) | copy-start | bytes 110596
  0.6 3.1 %copy-start = (bf16[8,24,8,256]{3,2,1,0:T(8,128)(2,1)S(1)}, bf16[8,24,8,256]{3,2,1,0:T(8,128)(2,1)}, u32[]{:S(2)}) copy-start(bf16[8,24,8,256]{3,2,1,0:T(8,128)(2,1)} %param.6) | copy-start | bytes 2359300
  3.6 0.9 %copy-start.2 = (bf16[64,64,3,3]{1,0,3,2:T(8,128)(2,1)S(1)}, bf16[64,64,3,3]{1,0,3,2:T(8,128)(2,1)}, u32[]{:S(2)}) copy-start(bf16[64,64,3,3]{1,0,3,2:T(8,128)(2,1)} %param.9) | copy-start | bytes 221188

commit v2 on v1

--- a/solution.py
+++ b/solution.py
@@ -45,6 +45,16 @@
     return ones_where(
         ((r >> 6) == ((c >> 7) & 1)) & ((c & 127) == 2 * (r & 63) + (c >> 8) - 1)
     )
+
+
+def stem_order(ah):
+    r, c = grid_of(C_IN * 16, 256)
+    return ones_where(r == (c & 31) * 16 + (2 * ah + (c >> 7)) * 4 + ((c >> 5) & 3))
+
+
+def stem_rows():
+    r, c = grid_of(C_IN * 16, 128)
+    return ones_where(c == (r & 3) * C_WIDE + (r >> 4))
 
 
 def dot(a, b, dims=((1,), (0,))):
@@ -82,12 +92,16 @@
 
 
 def kernel(
-    nl, nr, scen,
-    fields, ws, wm, wmb, wh, ow, pc,
-    pred, cot_out, g_stem, g_mid, g_head, g_out,
+    nl, nr,
+    fields, ws_hbm, wm_hbm, wh_hbm, ow_in, pc_in,
+    pred, cot_out, all_a, all_b,
+    ws, wm, wh,
     got, e_buf, a_rows, f_buf, v_buf, m_rows, col_r, cc, cot_send,
-    x_buf, half, got1, mine, got2, got3,
-    own_sem, sf, rf, sc, rc, s1, r1, s2, r2, s3, r3,
+    sum_a, half_a, one_a, mine_a, two_a,
+    sum_b, half_b, one_b, mine_b, two_b,
+    own_sem, w_sem, sf, rf, sc, rc,
+    s1a, r1a, s2a, r2a, s3a, r3a,
+    s1b, r1b, s2b, r2b, s3b, r3b,
 ):
     me, rep = lax.axis_index("lon"), lax.axis_index("rep")
     width = fields.shape[1] // C_IN
@@ -112,6 +126,11 @@
 
     own = pltpu.make_async_copy(fields.at[me], got.at[me], own_sem.at[0])
     own.start()
+    loads = []
+    for i, (src, dst) in enumerate(((ws_hbm, ws), (wm_hbm, wm), (wh_hbm, wh))):
+        load = pltpu.make_async_copy(src, dst, w_sem.at[i])
+        load.start()
+        loads.append(load)
     barrier = pltpu.get_barrier_semaphore()
     for k in range(1, nl):
         pl.semaphore_signal(barrier, inc=1, device_id=lon_peer(k), device_id_type=MESH)
@@ -126,6 +145,54 @@
             remote(fields.at[to], got.at[me], sf.at[k - 1], rf.at[k - 1], lon_peer(k))
         )
     sends += moved
+
+    def spread_out(x, y, sums, halves, one, send, recv):
+        x = jnp.concatenate([x, y], axis=1)
+        pad = sums.shape[0] - x.shape[0]
+        if pad:
+            x = jnp.concatenate([x, jnp.zeros((pad, 128), F32)], axis=0)
+        sums[...] = x
+        halves[...] = x.astype(BF16)
+        rows = sums.shape[0] // nl
+        copies = []
+        for k in range(1, nl):
+            to = pl.ds(pl.multiple_of(lax.rem(me + k, nl) * rows, 16), rows)
+            copies.append(
+                remote(halves.at[to], one.at[k - 1], send.at[k - 1], recv.at[k - 1], lon_peer(k))
+            )
+        return copies
+
+    def across(copies, sums, one, mine, two, send, recv):
+        rows = sums.shape[0] // nl
+        total = sums[pl.ds(pl.multiple_of(me * rows, 16), rows), :]
+        for k in range(1, nl):
+            copies[k - 1].wait_recv()
+            total = total + one[k - 1].astype(F32)
+        mine[...] = total.astype(BF16)
+        out = []
+        for k in range(1, nr):
+            out.append(remote(mine, two.at[rep], send.at[k - 1], recv.at[k - 1], rep_peer(k)))
+        two[rep] = mine[...]
+        return out
+
+    def gather(copies, two, everywhere, send, recv):
+        rows = everywhere.shape[0] // nl
+        for copy in copies:
+            copy.wait_recv()
+        total = two[0].astype(F32)
+        for k in range(1, nr):
+            total = total + two[k].astype(F32)
+        here = pl.ds(pl.multiple_of(me * rows, 16), rows)
+        everywhere[here, :] = total.astype(BF16)
+        out = []
+        for k in range(1, nl):
+            out.append(
+                remote(
+                    everywhere.at[here], everywhere.at[here],
+                    send.at[k - 1], recv.at[k - 1], lon_peer(k),
+                )
+            )
+        return out
 
     pick = stem_pick()
     order = slab_order(width)
@@ -150,7 +217,13 @@
     e_buf[0:128, 0:128] = e_buf[0:128, lonh * 128 :]
     e_buf[128:256, lonh * 128 :] = e_buf[128:256, 0:128]
 
-    both = dot(ws[...], e_buf[...])
+    for load in loads:
+        load.wait()
+    ws_rows = ws[...].astype(F32).reshape(C_IN * 16, C1).astype(BF16)
+    ws_all = jnp.concatenate(
+        [dot(ws_rows, stem_order(ah), ((0,), (0,))) for ah in range(2)], axis=0
+    ).astype(BF16)
+    both = dot(ws_all, e_buf[...])
     stem_pre = both[:C1, : lonh * 128] + both[C1:, 128:]
     stem_g = sigmoid(stem_pre)
     stem_act = (stem_pre * stem_g).astype(BF16)
@@ -190,9 +263,13 @@
         head_pre = s if head_pre is None else head_pre + s
     head_g = sigmoid(head_pre)
     head_act = (head_pre * head_g).astype(BF16).astype(F32)
-    pred[...] = jnp.sum(head_act * ow[...], axis=0, keepdims=True)
-    out_sum = jnp.sum(head_act * pc[...], axis=1, keepdims=True)
-    head_cot = (pc[...] * ow[...] * slope_of(head_pre, head_g)).astype(BF16).astype(F32)
+    r, c = grid_of(C2, C2)
+    ow = jnp.sum(jnp.where(r == c, ow_in[...], 0.0), axis=1, keepdims=True)
+    pc = jnp.concatenate([pc_in[0:tiles, :], pc_in[tiles:, :]], axis=1)
+    pc = jnp.concatenate([pc[t : t + 1, :] for t in range(tiles)], axis=1)
+    pred[...] = jnp.sum(head_act * ow, axis=0, keepdims=True)
+    out_sum = jnp.sum(head_act * pc, axis=1, keepdims=True)
+    head_cot = (pc * ow * slope_of(head_pre, head_g)).astype(BF16).astype(F32)
     for b in range(3):
         moved_lat = lat_shift(head_cot, 1 - b)
         for a in range(3):
@@ -204,6 +281,10 @@
 
     mid_sum_01 = dot(f_buf[:, 0:n], mid_cot, ((1,), (1,)))
     mid_sum_2 = dot(f_buf[0:96, 128 : n + 128], mid_cot, ((1,), (1,)))
+    block_a = jnp.concatenate(
+        [head_sum, jnp.broadcast_to(out_sum, (C2, C2)), mid_sum_01, mid_sum_2], axis=0
+    )
+    first_a = spread_out(block_a[:464], block_a[464:], sum_a, half_a, one_a, s1a, r1a)
     for t in range(tiles):
         m_rows[t * C2 : (t + 1) * C2, :] = mid_cot[:, t * 128 : (t + 1) * 128]
     up = dot(m_rows[...], mid_spread()).astype(BF16)
@@ -214,7 +295,17 @@
                 v_buf[b * C2 : (b + 1) * C2, lon * 128 : (lon + 1) * 128] = up[
                     t * C2 : (t + 1) * C2, b * 256 + q * 128 : b * 256 + (q + 1) * 128
                 ]
-    d = dot(wmb[...], v_buf[...])
+    wide = wm[...].astype(F32)
+    wmb = jnp.concatenate(
+        [
+            jnp.concatenate(
+                [wide[(a * 3 + b) * C1 : (a * 3 + b + 1) * C1] for a in range(3)], axis=0
+            )
+            for b in range(3)
+        ],
+        axis=1,
+    ).astype(BF16)
+    d = dot(wmb, v_buf[...])
     cc[0:C1, lonh * 128 :] = jnp.zeros((C1, 128), BF16)
     cc[C1 : 2 * C1, 0:128] = jnp.zeros((C1, 128), BF16)
     for i in range(lonh):
@@ -229,74 +320,52 @@
         cc[0:C1, i * 128 : (i + 1) * 128] = cot
         cc[C1 : 2 * C1, (i + 1) * 128 : (i + 2) * 128] = cot
         cot_send[i // per, :, (i % per) * 128 : (i % per + 1) * 128] = cot
+    second_a = across(first_a, sum_a, one_a, mine_a, two_a, s2a, r2a)
+    stem_sum = dot(e_buf[...], cc[...], ((1,), (1,)))
+    first_b = spread_out(stem_sum[:128], stem_sum[128:], sum_b, half_b, one_b, s1b, r1b)
+    third_a = gather(second_a, two_a, all_a, s3a, r3a)
     back = []
     for k in range(1, nl):
         to = lax.rem(me + k, nl)
         back.append(
             remote(cot_send.at[to], cot_out.at[me], sc.at[k - 1], rc.at[k - 1], lon_peer(k))
         )
-    sends += back
     own_back = pltpu.make_async_copy(cot_send.at[me], cot_out.at[me], own_sem.at[1])
     own_back.start()
-    stem_sum = dot(e_buf[...], cc[...], ((1,), (1,)))
-
-    total_rows = x_buf.shape[0]
-    rows = total_rows // nl
-    left = [head_sum, jnp.broadcast_to(out_sum, (C2, C2))]
-    right = [mid_sum_01, mid_sum_2, stem_sum]
-    if total_rows > 640:
-        left.append(jnp.zeros((total_rows - 640, 64), F32))
-    right.append(jnp.zeros((total_rows - 544, 64), F32))
-    x = jnp.concatenate(
-        [jnp.concatenate(left, axis=0), jnp.concatenate(right, axis=0)], axis=1
-    )
-    x_buf[...] = x
-    half[...] = x.astype(BF16)
-
-    def part_of(at):
-        return pl.ds(pl.multiple_of(at * rows, 16), rows)
-
-    first = []
-    for k in range(1, nl):
-        to = lax.rem(me + k, nl)
-        first.append(
-            remote(half.at[part_of(to)], got1.at[k - 1], s1.at[k - 1], r1.at[k - 1], lon_peer(k))
-        )
-    total = x_buf[part_of(me), :]
-    for k in range(1, nl):
-        first[k - 1].wait_recv()
-        total = total + got1[k - 1].astype(F32)
-    mine[...] = total.astype(BF16)
-    second = []
-    for k in range(1, nr):
-        second.append(remote(mine, got2.at[rep], s2.at[k - 1], r2.at[k - 1], rep_peer(k)))
-    got2[rep] = mine[...]
-    for copy in second:
+    second_b = across(first_b, sum_b, one_b, mine_b, two_b, s2b, r2b)
+    third_b = gather(second_b, two_b, all_b, s3b, r3b)
+    for copy in third_a + back + third_b:
         copy.wait_recv()
-    total = got2[0].astype(F32)
-    for k in range(1, nr):
-        total = total + got2[k].astype(F32)
-    got3[part_of(me), :] = total.astype(BF16)
-    third = []
-    for k in range(1, nl):
-        third.append(
-            remote(
-                got3.at[part_of(me)], got3.at[part_of(me)], s3.at[k - 1], r3.at[k - 1], lon_peer(k)
-            )
-        )
-    for copy in third:
-        copy.wait_recv()
-    factor = 1.0 / scen
-    summed = got3[...].astype(F32) * factor
-    g_head[...] = summed[0:576, 0:64]
-    g_out[...] = summed[576:640, 0:1]
-    g_mid[...] = summed[0:288, 64:128]
-    g_stem[...] = summed[288:544, 64:128]
     own_back.wait()
-    for copy in back:
-        copy.wait_recv()
-    for copy in sends + first + second + third:
+    for copy in moved + first_a + second_a + third_a + back + first_b + second_b + third_b:
         copy.wait_send()
+
+
+def finish(factor, pred, cot, all_a, all_b, pred_out, cot_out, g_stem, g_mid, g_head, g_out):
+    tiles = pred.shape[1] // 128
+    lines = jnp.concatenate(
+        [pred[:, t * 128 : (t + 1) * 128] for t in range(tiles)], axis=0
+    )
+    pred_out[0:tiles, :] = lines[:, 0:64]
+    pred_out[tiles:, :] = lines[:, 64:128]
+    a = all_a[0:464, :].astype(F32) * factor
+    g_head[0:464, :] = a[:, 0:64]
+    g_head[464:576, :] = a[0:112, 64:128]
+    r, c = grid_of(C2, C2)
+    g_out[...] = jnp.sum(
+        jnp.where(r == c, a[112:176, 64:128], 0.0), axis=0, keepdims=True
+    )
+    g_mid[...] = a[176:464, 64:128]
+    rows = dot(stem_rows(), all_b[0:128, :])
+    r, c = grid_of(C_IN * 16, 128)
+    group = (r >> 2) & 3
+    kept = jnp.where((c >> 5) == (group & 1) * 2 + (group >> 1), rows, 0.0).astype(BF16)
+    r, c = grid_of(128, C1)
+    stem = dot(kept, ones_where((r & 31) == c)) * factor
+    g_stem[...] = stem.reshape(g_stem.shape)
+    for s in range(cot.shape[0]):
+        whole = cot[s].astype(F32)
+        cot_out[s] = whole.reshape(cot_out.shape[1:]).astype(BF16)
 
 
 def local(nl, nr, fields, stem_weight, mid_weight, head_weight, out_weight, pred_cotangent):
@@ -305,30 +374,43 @@
     lonh = nl * per
     tiles = lonh // 4
     lonc = 2 * tiles
-    x_rows = -(-640 // (nl * 16)) * nl * 16
-    rows = x_rows // nl
-    ws = jnp.pad(stem_weight, ((0, 0), (0, C_WIDE - C_IN), (0, 0), (0, 0)))
-    ws = ws.reshape(C1, C_WIDE, 2, 2, 4).transpose(2, 0, 3, 4, 1).reshape(2 * C1, 256)
+    ws = stem_weight.transpose(1, 2, 3, 0).reshape(C_IN * 4, 4, C1)
     wm = mid_weight.transpose(2, 3, 1, 0).reshape(288, C2)
-    wmb = mid_weight.transpose(2, 1, 3, 0).reshape(96, 192)
     wh = head_weight.transpose(2, 3, 0, 1).reshape(576, C2)
-    pc = pred_cotangent.reshape(2, tiles, 64).transpose(1, 0, 2).reshape(1, tiles * 128)
     vmem = pl.BlockSpec(memory_space=pltpu.VMEM)
-    hbm = pl.BlockSpec(memory_space=pl.ANY)
+    hbm = pl.BlockSpec(memory_space=pltpu.HBM)
     dma = pltpu.SemaphoreType.DMA
-    pred, cot, g_stem, g_mid, g_head, g_out = pl.pallas_call(
-        functools.partial(kernel, nl, nr, scen_here * nr),
+
+    def sum_scratch(size):
+        return [
+            pltpu.VMEM((size, 128), F32),
+            pltpu.VMEM((size, 128), BF16),
+            pltpu.VMEM((nl - 1, size // nl, 128), BF16),
+            pltpu.VMEM((size // nl, 128), BF16),
+            pltpu.VMEM((nr, size // nl, 128), BF16),
+        ]
+
+    sum_sems = [
+        dma((nl - 1,)), dma((nl - 1,)),
+        dma((nr - 1,)), dma((nr - 1,)),
+        dma((nl - 1,)), dma((nl - 1,)),
+    ]
+    size_a = -(-464 // (nl * 16)) * nl * 16
+    size_b = -(-128 // (nl * 16)) * nl * 16
+    pred, cot, all_a, all_b = pl.pallas_call(
+        functools.partial(kernel, nl, nr),
         out_shape=[
             jax.ShapeDtypeStruct((1, tiles * 128), F32),
             jax.ShapeDtypeStruct((nl, C1, per * 128), BF16),
-            jax.ShapeDtypeStruct((256, C2), F32),
-            jax.ShapeDtypeStruct((288, C2), F32),
-            jax.ShapeDtypeStruct((576, C2), F32),
-            jax.ShapeDtypeStruct((C2, 1), F32),
+            jax.ShapeDtypeStruct((size_a, 128), BF16),
+            jax.ShapeDtypeStruct((size_b, 128), BF16),
         ],
-        in_specs=[hbm] + [vmem] * 6,
-        out_specs=[vmem, hbm, vmem, vmem, vmem, vmem],
+        in_specs=[hbm] * 4 + [vmem] * 2,
+        out_specs=[vmem] * 4,
         scratch_shapes=[
+            pltpu.VMEM(ws.shape, BF16),
+            pltpu.VMEM(wm.shape, BF16),
+            pltpu.VMEM(wh.shape, BF16),
             pltpu.VMEM((nl, C_IN * width, lat), BF16),
             pltpu.VMEM((256, (lonh + 1) * 128), BF16),
             pltpu.VMEM((lonh // 2 * C1, 256), BF16),
@@ -338,33 +420,44 @@
             pltpu.VMEM((576, tiles * 128), BF16),
             pltpu.VMEM((2 * C1, (lonh + 1) * 128), BF16),
             pltpu.VMEM((nl, C1, per * 128), BF16),
-            pltpu.VMEM((x_rows, 128), F32),
-            pltpu.VMEM((x_rows, 128), BF16),
-            pltpu.VMEM((nl - 1, rows, 128), BF16),
-            pltpu.VMEM((rows, 128), BF16),
-            pltpu.VMEM((nr, rows, 128), BF16),
-            pltpu.VMEM((x_rows, 128), BF16),
-            dma((2,)),
+        ]
+        + sum_scratch(size_a)
+        + sum_scratch(size_b)
+        + [
+            dma((2,)), dma((3,)),
             dma((nl - 1,)), dma((nl - 1,)),
             dma((nl - 1,)), dma((nl - 1,)),
-            dma((nl - 1,)), dma((nl - 1,)),
-            dma((nr - 1,)), dma((nr - 1,)),
-            dma((nl - 1,)), dma((nl - 1,)),
-        ],
+        ]
+        + sum_sems
+        + sum_sems,
         compiler_params=pltpu.CompilerParams(
-            collective_id=0, has_side_effects=True, vmem_limit_bytes=50 * 2**20
+            collective_id=0, has_side_effects=True, vmem_limit_bytes=48 * 2**20
         ),
     )(
         fields.reshape(scen_here, C_IN * width, lat),
-        ws, wm, wmb, wh, out_weight.reshape(C2, 1), pc,
-    )
-    prediction = pred.reshape(tiles, 2, 64).transpose(1, 0, 2).reshape(1, lonc, 64)
-    stem_cotangent = cot.reshape(nl, C1, per, 128)
-    grad_stem = g_stem.reshape(2, 4, C_WIDE, 2, C1)[:, :, :C_IN].transpose(4, 2, 3, 0, 1)
-    grad_stem = grad_stem.reshape(C1, C_IN, 4, 4)
+        ws, wm, wh, out_weight.reshape(1, C2), pred_cotangent.reshape(lonc, 64),
+    )
+    prediction, stem_cotangent, g_stem, g_mid, g_head, g_out = pl.pallas_call(
+        functools.partial(finish, 1.0 / (scen_here * nr)),
+        out_shape=[
+            jax.ShapeDtypeStruct((lonc, 64), F32),
+            jax.ShapeDtypeStruct((nl, C1, per, 128), BF16),
+            jax.ShapeDtypeStruct((C_IN * 4, 4, C1), F32),
+            jax.ShapeDtypeStruct((288, C2), F32),
+            jax.ShapeDtypeStruct((576, C2), F32),
+            jax.ShapeDtypeStruct((1, C2), F32),
+        ],
+        in_specs=[vmem] * 4,
+        out_specs=[vmem] * 6,
+        compiler_params=pltpu.CompilerParams(vmem_limit_bytes=32 * 2**20),
+    )(pred, cot, all_a, all_b)
+    grad_stem = g_stem.reshape(C_IN, 4, 4, C1).transpose(3, 0, 1, 2)
     grad_mid = g_mid.reshape(3, 3, C1, C2).transpose(3, 2, 0, 1)
     grad_head = g_head.reshape(3, 3, C2, C2).transpose(2, 3, 0, 1)
-    return prediction, stem_cotangent, grad_stem, grad_mid, grad_head, g_out.reshape(C2)
+    return (
+        prediction.reshape(1, lonc, 64), stem_cotangent,
+        grad_stem, grad_mid, grad_head, g_out.reshape(C2),
+    )
 
 
 def solution(mesh):

time: 44.8 us -> 41.9 us (0.935)
  local copies, waits for them, and re-layouts: 8.29 us -> 4.5 us
  Pallas kernels: 34.3 us -> 36.5 us
  other arithmetic: 1.29 us -> 0 us
    reshape x9 -> x0, local copies, waits for them, and re-layouts: 3.06 us -> none  [the longest x2 0.87 us: local(): pred_cotangent.reshape(2, tiles, 64).transpose(1, 0, 2)]
    pallas_call x1 -> x2, Pallas kernels: 34.3 us -> 36.5 us  [the longest x1 35.3 us: local(): pl.pallas_call(functools.partial(kernel, nl, nr), out_shape=[jax.ShapeDty...]
    unnamed x9 -> x12, local copies, waits for them, and re-layouts: 2.89 us -> 4.5 us
    pallas_call x2 -> x0, other arithmetic: 1.29 us -> none  [local(): pl.pallas_call(functools.partial(kernel, nl, nr, scen_here * nr), out_sha...]
    pad x1 -> x0, local copies, waits for them, and re-layouts: 0.95 us -> none  [local(): ws = jnp.pad(stem_weight, ((0, 0), (0, C_WIDE - C_IN), (0, 0), (0, 0)))]
    transpose x4 -> x0, local copies, waits for them, and re-layouts: 0.8 us -> none  [the longest x1 0.6 us: local(): pred.reshape(tiles, 2, 64).transpose(1, 0, 2).reshape(1, lonc, 64)]
    pallas_call x2 -> x0, local copies, waits for them, and re-layouts: 0.59 us -> none  [local(): pl.pallas_call(functools.partial(kernel, nl, nr, scen_here * nr), out_sha...]
where the time goes in v2:
time: 41.9 us; the launch traced here: 41.6 us
  Pallas kernels  36.5 us (87%)
  local copies, waits for them, and re-layouts  4.5 us (11%)
  between operations  0.66 us (2%)
    pallas_call x1, Pallas kernels, local(): pl.pallas_call(functools.partial(kernel, nl, nr), out_shape=[jax.ShapeDty...  35.3 us
    unnamed x12, local copies, waits for them, and re-layouts  4.5 us
    pallas_call x1, Pallas kernels, local(): pl.pallas_call(functools.partial(finish, 1.0 / (scen_here * nr)), out_sha...  1.15 us

profile of v2, /device:TPU:0, one launch (start us, length us, event | category | flops | bytes accessed | tf_op | source)
XLA Modules:
  0.0 41.6 jit_solution(18192106059953664299)
XLA Ops:
  0.6 0.0 copy-start.4
  0.6 0.0 copy-start.5
  0.7 0.7 %copy-done.4 = f32[1,16,64]{2,1,0:T(8,128)S(1)} copy-done((f32[1,16,64]{2,1,0:T(8,128)S(1)}, f32[1,16,64]{2,1,0:T(8,128)}, u32[]{:S(2)}) %copy-start.4) | copy-done | bytes 4120
  1.3 0.0 copy-done.5
  1.3 0.0 copy-start
  1.3 1.1 %copy-done = bf16[8,24,8,256]{3,2,1,0:T(8,128)(2,1)S(1)} copy-done((bf16[8,24,8,256]{3,2,1,0:T(8,128)(2,1)S(1)}, bf16[8,24,8,256]{3,2,1,0:T(8,128)(2,1)}, u32[]{:S(2)}) %copy-start) | copy-done | bytes 786456
  2.5 0.0 copy-start.1
  2.5 0.9 %copy-done.1 = bf16[64,64,3,3]{1,0,3,2:T(8,128)(2,1)S(1)} copy-done((bf16[64,64,3,3]{1,0,3,2:T(8,128)(2,1)S(1)}, bf16[64,64,3,3]{1,0,3,2:T(8,128)(2,1)}, u32[]{:S(2)}) %copy-start.1) | copy-done | bytes 73752
  3.4 0.0 copy-start.2
  3.4 0.9 %copy-done.2 = bf16[32,24,4,4]{0,3,2,1:T(4,128)(2,1)S(1)} copy-done((bf16[32,24,4,4]{0,3,2,1:T(4,128)(2,1)S(1)}, bf16[32,24,4,4]{0,3,2,1:T(4,128)(2,1)}, u32[]{:S(2)}) %copy-start.2) | copy-done | bytes 24600
  4.3 0.0 copy-start.3
  4.3 0.9 %copy-done.3 = bf16[64,32,3,3]{0,1,3,2:T(8,128)(2,1)S(1)} copy-done((bf16[64,32,3,3]{0,1,3,2:T(8,128)(2,1)S(1)}, bf16[64,32,3,3]{0,1,3,2:T(8,128)(2,1)}, u32[]{:S(2)}) %copy-start.3) | copy-done | bytes 36888
  5.2 35.3 %shard_map.109 = (f32[1,1024]{1,0:T(1,128)S(1)}, bf16[8,32,512]{2,1,0:T(8,128)(2,1)S(1)}, bf16[512,128]{1,0:T(8,128)(2,1)S(1)}, bf16[128,128]{1,0:T(8,128)(2,1)S(1)}) custom-call(bf16[8,192,256]{2,1,0:T(8,128)(2,1)S(1)} %bitcast.23, bf16[96,4,32]{2,1,0:T(4,128)(2,1)S(1)} %bitcast.25, bf16[288,64]{1,0:T(8,128)(2,1)S(1)} %bitcast.26, ...), custom_call_target="tpu_custom_call" | custom-call | tf_op jit(solution)/shard_map/pallas_call | solution.py:400
  40.5 1.2 %shard_map.110 = (f32[16,64]{1,0:T(8,128)}, bf16[8,32,4,128]{3,2,1,0:T(4,128)(2,1)}, f32[96,4,32]{2,1,0:T(4,128)}, f32[288,64]{1,0:T(8,128)}, f32[576,64]{1,0:T(8,128)}, /*index=5*/f32[1,64]{1,0:T(1,128)}) custom-call(f32[1,1024]{1,0:T(1,128)S(1)} %get-tuple-element.16.pred, bf16[8,32,512]{2,1,0:T(8,128)(2,1)S(1)} %get-tuple-element.17.cot, ...), custom_call_target="tpu_custom_call" | custom-call | tf_op jit(solution)/shard_map/pallas_call | solution.py:440
Async XLA Ops:
  0.6 0.7 %copy-start.4 = (f32[1,16,64]{2,1,0:T(8,128)S(1)}, f32[1,16,64]{2,1,0:T(8,128)}, u32[]{:S(2)}) copy-start(f32[1,16,64]{2,1,0:T(8,128)} %param.11) | copy-start | bytes 12292
  0.6 0.7 %copy-start.5 = (f32[64]{0:T(128)S(1)}, f32[64]{0:T(128)}, u32[]{:S(2)}) copy-start(f32[64]{0:T(128)} %param.10) | copy-start | bytes 772
  1.3 1.1 %copy-start = (bf16[8,24,8,256]{3,2,1,0:T(8,128)(2,1)S(1)}, bf16[8,24,8,256]{3,2,1,0:T(8,128)(2,1)}, u32[]{:S(2)}) copy-start(bf16[8,24,8,256]{3,2,1,0:T(8,128)(2,1)} %param.6) | copy-start | bytes 2359300
  2.5 0.9 %copy-start.1 = (bf16[64,64,3,3]{1,0,3,2:T(8,128)(2,1)S(1)}, bf16[64,64,3,3]{1,0,3,2:T(8,128)(2,1)}, u32[]{:S(2)}) copy-start(bf16[64,64,3,3]{1,0,3,2:T(8,128)(2,1)} %param.9) | copy-start | bytes 221188
  3.4 0.9 %copy-start.2 = (bf16[32,24,4,4]{0,3,2,1:T(4,128)(2,1)S(1)}, bf16[32,24,4,4]{0,3,2,1:T(4,128)(2,1)}, u32[]{:S(2)}) copy-start(bf16[32,24,4,4]{0,3,2,1:T(4,128)(2,1)} %param.7) | copy-start | bytes 73732
  4.3 0.9 %copy-start.3 = (bf16[64,32,3,3]{0,1,3,2:T(8,128)(2,1)S(1)}, bf16[64,32,3,3]{0,1,3,2:T(8,128)(2,1)}, u32[]{:S(2)}) copy-start(bf16[64,32,3,3]{0,1,3,2:T(8,128)(2,1)} %param.8) | copy-start | bytes 110596

commit v3 on v2

--- a/solution.py
+++ b/solution.py
@@ -93,9 +93,10 @@
 
 def kernel(
     nl, nr,
-    fields, ws_hbm, wm_hbm, wh_hbm, ow_in, pc_in,
+    fields, ws_hbm, wm_hbm, wh_hbm, ow_hbm, pc_hbm,
     pred, cot_out, all_a, all_b,
-    ws, wm, wh,
+    ws, wm, wh, ow_in, pc_in,
+    ws_all, wmb, pick_mid, spread_mid, y_buf,
     got, e_buf, a_rows, f_buf, v_buf, m_rows, col_r, cc, cot_send,
     sum_a, half_a, one_a, mine_a, two_a,
     sum_b, half_b, one_b, mine_b, two_b,
@@ -127,7 +128,7 @@
     own = pltpu.make_async_copy(fields.at[me], got.at[me], own_sem.at[0])
     own.start()
     loads = []
-    for i, (src, dst) in enumerate(((ws_hbm, ws), (wm_hbm, wm), (wh_hbm, wh))):
+    for i, (src, dst) in enumerate(((ws_hbm, ws), (wm_hbm, wm), (wh_hbm, wh), (ow_hbm, ow_in), (pc_hbm, pc_in))):
         load = pltpu.make_async_copy(src, dst, w_sem.at[i])
         load.start()
         loads.append(load)
@@ -194,8 +195,33 @@
             )
         return out
 
+    for load in loads:
+        load.wait()
+    ws_rows = ws[...].astype(F32).reshape(C_IN * 16, C1).astype(BF16)
+    for ah in range(2):
+        ws_all[ah * C1 : (ah + 1) * C1, :] = dot(
+            ws_rows, stem_order(ah), ((0,), (0,))
+        ).astype(BF16)
+    wide = wm[...].astype(F32)
+    wmb[...] = jnp.concatenate(
+        [
+            jnp.concatenate(
+                [wide[(a * 3 + b) * C1 : (a * 3 + b + 1) * C1] for a in range(3)], axis=0
+            )
+            for b in range(3)
+        ],
+        axis=1,
+    ).astype(BF16)
+    pick_mid[...] = mid_pick()
+    spread_mid[...] = mid_spread()
     pick = stem_pick()
     order = slab_order(width)
+    group = per * 128
+
+    def stem_group(g):
+        where = pl.ds(pl.multiple_of(g * group, 128), group)
+        y_buf[:, where] = dot(ws_all[...], e_buf[:, where])
+
     for k in range(nl):
         if k == 0:
             own.wait()
@@ -206,25 +232,24 @@
         lines = dot(order, got[source]).astype(BF16)
         taps = dot(lines, pick).astype(BF16)
         for l in range(width):
-            at = (l % 2 == 0)
-            tile = source * per + l // 2 + (0 if at else 1)
+            even = l % 2 == 0
+            tile = source * per + l // 2 - (1 if even else 0)
+            if l == 0:
+                tile = lax.rem(tile + lonh, lonh)
             where = pl.ds(pl.multiple_of(tile * 128, 128), 128)
             for b in range(4):
-                row = (128 if at else 0) + b * C_WIDE
+                row = (128 if even else 0) + b * C_WIDE
                 e_buf[row : row + C_WIDE, where] = taps[
                     l * C_WIDE : (l + 1) * C_WIDE, b * 128 : (b + 1) * 128
                 ]
-    e_buf[0:128, 0:128] = e_buf[0:128, lonh * 128 :]
-    e_buf[128:256, lonh * 128 :] = e_buf[128:256, 0:128]
-
-    for load in loads:
-        load.wait()
-    ws_rows = ws[...].astype(F32).reshape(C_IN * 16, C1).astype(BF16)
-    ws_all = jnp.concatenate(
-        [dot(ws_rows, stem_order(ah), ((0,), (0,))) for ah in range(2)], axis=0
-    ).astype(BF16)
-    both = dot(ws_all, e_buf[...])
-    stem_pre = both[:C1, : lonh * 128] + both[C1:, 128:]
+        if k > 0:
+            stem_group(source)
+    stem_group(me)
+
+    last = (lonh - 1) * 128
+    stem_pre = (
+        jnp.concatenate([y_buf[0:C1, last:], y_buf[0:C1, :last]], axis=1) + y_buf[C1:, :]
+    )
     stem_g = sigmoid(stem_pre)
     stem_act = (stem_pre * stem_g).astype(BF16)
     stem_slope = slope_of(stem_pre, stem_g)
@@ -232,7 +257,7 @@
     for l in range(hl):
         a_rows[l * C1 : (l + 1) * C1, 0:128] = stem_act[:, l * 128 : (l + 1) * 128]
         a_rows[l * C1 : (l + 1) * C1, 128:256] = stem_act[:, (l + hl) * 128 : (l + hl + 1) * 128]
-    u = dot(a_rows[...], mid_pick())
+    u = dot(a_rows[...], pick_mid[...])
     ub = u.astype(BF16)
     for b in range(3):
         last = u[(hl - 1) * C1 : hl * C1, b * 128 : (b + 1) * 128]
@@ -287,7 +312,7 @@
     first_a = spread_out(block_a[:464], block_a[464:], sum_a, half_a, one_a, s1a, r1a)
     for t in range(tiles):
         m_rows[t * C2 : (t + 1) * C2, :] = mid_cot[:, t * 128 : (t + 1) * 128]
-    up = dot(m_rows[...], mid_spread()).astype(BF16)
+    up = dot(m_rows[...], spread_mid[...]).astype(BF16)
     for t in range(tiles):
         for b in range(3):
             for q in range(2):
@@ -295,19 +320,7 @@
                 v_buf[b * C2 : (b + 1) * C2, lon * 128 : (lon + 1) * 128] = up[
                     t * C2 : (t + 1) * C2, b * 256 + q * 128 : b * 256 + (q + 1) * 128
                 ]
-    wide = wm[...].astype(F32)
-    wmb = jnp.concatenate(
-        [
-            jnp.concatenate(
-                [wide[(a * 3 + b) * C1 : (a * 3 + b + 1) * C1] for a in range(3)], axis=0
-            )
-            for b in range(3)
-        ],
-        axis=1,
-    ).astype(BF16)
-    d = dot(wmb, v_buf[...])
-    cc[0:C1, lonh * 128 :] = jnp.zeros((C1, 128), BF16)
-    cc[C1 : 2 * C1, 0:128] = jnp.zeros((C1, 128), BF16)
+    d = dot(wmb[...], v_buf[...])
     for i in range(lonh):
         m = i // 2
         if i % 2 == 0:
@@ -317,8 +330,9 @@
             grad = d[2 * C1 :, m * 128 : (m + 1) * 128] + d[:C1, nxt * 128 : (nxt + 1) * 128]
         cot = grad.astype(BF16).astype(F32) * stem_slope[:, i * 128 : (i + 1) * 128]
         cot = cot.astype(BF16)
-        cc[0:C1, i * 128 : (i + 1) * 128] = cot
-        cc[C1 : 2 * C1, (i + 1) * 128 : (i + 2) * 128] = cot
+        before = (i - 1) % lonh
+        cc[0:C1, before * 128 : (before + 1) * 128] = cot
+        cc[C1 : 2 * C1, i * 128 : (i + 1) * 128] = cot
         cot_send[i // per, :, (i % per) * 128 : (i % per + 1) * 128] = cot
     second_a = across(first_a, sum_a, one_a, mine_a, two_a, s2a, r2a)
     stem_sum = dot(e_buf[...], cc[...], ((1,), (1,)))
@@ -332,12 +346,18 @@
         )
     own_back = pltpu.make_async_copy(cot_send.at[me], cot_out.at[me], own_sem.at[1])
     own_back.start()
+    for copy in moved + first_a:
+        copy.wait_send()
     second_b = across(first_b, sum_b, one_b, mine_b, two_b, s2b, r2b)
+    for copy in second_a + third_a:
+        copy.wait_send()
     third_b = gather(second_b, two_b, all_b, s3b, r3b)
+    own_back.wait()
+    for copy in first_b + second_b:
+        copy.wait_send()
     for copy in third_a + back + third_b:
         copy.wait_recv()
-    own_back.wait()
-    for copy in moved + first_a + second_a + third_a + back + first_b + second_b + third_b:
+    for copy in back + third_b:
         copy.wait_send()
 
 
@@ -405,33 +425,40 @@
             jax.ShapeDtypeStruct((size_a, 128), BF16),
             jax.ShapeDtypeStruct((size_b, 128), BF16),
         ],
-        in_specs=[hbm] * 4 + [vmem] * 2,
-        out_specs=[vmem] * 4,
+        in_specs=[hbm] * 6,
+        out_specs=[vmem, hbm, vmem, vmem],
         scratch_shapes=[
             pltpu.VMEM(ws.shape, BF16),
             pltpu.VMEM(wm.shape, BF16),
             pltpu.VMEM(wh.shape, BF16),
+            pltpu.VMEM((1, C2), F32),
+            pltpu.VMEM((lonc, 64), F32),
+            pltpu.VMEM((2 * C1, 256), BF16),
+            pltpu.VMEM((96, 192), BF16),
+            pltpu.VMEM((256, 384), BF16),
+            pltpu.VMEM((128, 768), BF16),
+            pltpu.VMEM((2 * C1, lonh * 128), F32),
             pltpu.VMEM((nl, C_IN * width, lat), BF16),
-            pltpu.VMEM((256, (lonh + 1) * 128), BF16),
+            pltpu.VMEM((256, lonh * 128), BF16),
             pltpu.VMEM((lonh // 2 * C1, 256), BF16),
             pltpu.VMEM((192, (tiles + 1) * 128), BF16),
             pltpu.VMEM((192, lonc * 128), BF16),
             pltpu.VMEM((tiles * C2, 128), BF16),
             pltpu.VMEM((576, tiles * 128), BF16),
-            pltpu.VMEM((2 * C1, (lonh + 1) * 128), BF16),
+            pltpu.VMEM((2 * C1, lonh * 128), BF16),
             pltpu.VMEM((nl, C1, per * 128), BF16),
         ]
         + sum_scratch(size_a)
         + sum_scratch(size_b)
         + [
-            dma((2,)), dma((3,)),
+            dma((2,)), dma((5,)),
             dma((nl - 1,)), dma((nl - 1,)),
             dma((nl - 1,)), dma((nl - 1,)),
         ]
         + sum_sems
         + sum_sems,
         compiler_params=pltpu.CompilerParams(
-            collective_id=0, has_side_effects=True, vmem_limit_bytes=48 * 2**20
+            collective_id=0, has_side_effects=True, vmem_limit_bytes=60 * 2**20
         ),
     )(
         fields.reshape(scen_here, C_IN * width, lat),
@@ -449,7 +476,7 @@
         ],
         in_specs=[vmem] * 4,
         out_specs=[vmem] * 6,
-        compiler_params=pltpu.CompilerParams(vmem_limit_bytes=32 * 2**20),
+        compiler_params=pltpu.CompilerParams(vmem_limit_bytes=60 * 2**20),
     )(pred, cot, all_a, all_b)
     grad_stem = g_stem.reshape(C_IN, 4, 4, C1).transpose(3, 0, 1, 2)
     grad_mid = g_mid.reshape(3, 3, C1, C2).transpose(3, 2, 0, 1)

time: 41.9 us -> 38.8 us (0.926)
  local copies, waits for them, and re-layouts: 4.5 us -> 0 us
  Pallas kernels: 36.5 us -> 38 us
    unnamed x12 -> x0, local copies, waits for them, and re-layouts: 4.5 us -> none
    pallas_call x1, Pallas kernels: 1.15 us -> 2.14 us  [local(): pl.pallas_call(functools.partial(finish, 1.0 / (scen_here * nr)), out_sha...]
    pallas_call x1, Pallas kernels: 35.3 us -> 35.9 us  [local(): pl.pallas_call(functools.partial(kernel, nl, nr), out_shape=[jax.ShapeDty...]
where the time goes in v3:
time: 38.8 us; the launch traced here: 38.6 us
  Pallas kernels  38 us (98%)
  between operations  0.64 us (2%)
    pallas_call x1, Pallas kernels, local(): pl.pallas_call(functools.partial(kernel, nl, nr), out_shape=[jax.ShapeDty...  35.9 us
    pallas_call x1, Pallas kernels, local(): pl.pallas_call(functools.partial(finish, 1.0 / (scen_here * nr)), out_sha...  2.14 us

profile of v3, /device:TPU:0, one launch (start us, length us, event | category | flops | bytes accessed | tf_op | source)
XLA Modules:
  0.0 38.6 jit_solution(9060072407882696400)
XLA Ops:
  0.6 35.9 %shard_map.109 = (f32[1,1024]{1,0:T(1,128)}, bf16[8,32,512]{2,1,0:T(8,128)(2,1)}, bf16[512,128]{1,0:T(8,128)(2,1)}, bf16[128,128]{1,0:T(8,128)(2,1)}) custom-call(bf16[8,192,256]{2,1,0:T(8,128)(2,1)} %bitcast.23, bf16[96,4,32]{2,1,0:T(4,128)(2,1)} %bitcast.25, bf16[288,64]{1,0:T(8,128)(2,1)} %bitcast.26, bf16[576,64]{1,0:T(8,128)(2,1)} %bitcast.24, ...), custom_call_target="tpu_custom_call" | custom-call | tf_op jit(solution)/shard_map/pallas_call | solution.py:420
  36.5 2.1 %shard_map.110 = (f32[16,64]{1,0:T(8,128)}, bf16[8,32,4,128]{3,2,1,0:T(4,128)(2,1)}, f32[96,4,32]{2,1,0:T(4,128)}, f32[288,64]{1,0:T(8,128)}, f32[576,64]{1,0:T(8,128)}, /*index=5*/f32[1,64]{1,0:T(1,128)}) custom-call(f32[1,1024]{1,0:T(1,128)} %get-tuple-element.16.pred, bf16[8,32,512]{2,1,0:T(8,128)(2,1)} %get-tuple-element.17.cot, ...), custom_call_target="tpu_custom_call" | custom-call | tf_op jit(solution)/shard_map/pallas_call | solution.py:467

commit v4 on v3

--- a/solution.py
+++ b/solution.py
@@ -62,7 +62,7 @@
 
 
 def sigmoid(v):
-    return 1.0 / (1.0 + jnp.exp(-v))
+    return 0.5 + 0.5 * jnp.tanh(0.5 * v)
 
 
 def slope_of(v, g):
@@ -96,7 +96,7 @@
     fields, ws_hbm, wm_hbm, wh_hbm, ow_hbm, pc_hbm,
     pred, cot_out, all_a, all_b,
     ws, wm, wh, ow_in, pc_in,
-    ws_all, wmb, pick_mid, spread_mid, y_buf,
+    ws_all, wmb, pick_mid, spread_mid, y_buf, slopes,
     got, e_buf, a_rows, f_buf, v_buf, m_rows, col_r, cc, cot_send,
     sum_a, half_a, one_a, mine_a, two_a,
     sum_b, half_b, one_b, mine_b, two_b,
@@ -222,6 +222,19 @@
         where = pl.ds(pl.multiple_of(g * group, 128), group)
         y_buf[:, where] = dot(ws_all[...], e_buf[:, where])
 
+    def act_group(g):
+        for i in range(per):
+            tile = g * per + i
+            here = pl.ds(pl.multiple_of(tile * 128, 128), 128)
+            prior = lax.rem(tile - 1 + lonh, lonh) if i == 0 else tile - 1
+            prior = pl.ds(pl.multiple_of(prior * 128, 128), 128)
+            pre = y_buf[0:C1, prior] + y_buf[C1:, here]
+            gate = sigmoid(pre)
+            slopes[:, here] = slope_of(pre, gate)
+            line = pl.ds(pl.multiple_of(lax.rem(tile, hl) * C1, C1), C1)
+            half = pl.ds(pl.multiple_of(lax.div(tile, hl) * 128, 128), 128)
+            a_rows[line, half] = (pre * gate).astype(BF16)
+
     for k in range(nl):
         if k == 0:
             own.wait()
@@ -244,19 +257,12 @@
                 ]
         if k > 0:
             stem_group(source)
+        if k > 1:
+            act_group(lax.rem(source + 1, nl))
     stem_group(me)
-
-    last = (lonh - 1) * 128
-    stem_pre = (
-        jnp.concatenate([y_buf[0:C1, last:], y_buf[0:C1, :last]], axis=1) + y_buf[C1:, :]
-    )
-    stem_g = sigmoid(stem_pre)
-    stem_act = (stem_pre * stem_g).astype(BF16)
-    stem_slope = slope_of(stem_pre, stem_g)
-
-    for l in range(hl):
-        a_rows[l * C1 : (l + 1) * C1, 0:128] = stem_act[:, l * 128 : (l + 1) * 128]
-        a_rows[l * C1 : (l + 1) * C1, 128:256] = stem_act[:, (l + hl) * 128 : (l + hl + 1) * 128]
+    act_group(lax.rem(me + 1, nl))
+    act_group(me)
+
     u = dot(a_rows[...], pick_mid[...])
     ub = u.astype(BF16)
     for b in range(3):
@@ -321,6 +327,7 @@
                     t * C2 : (t + 1) * C2, b * 256 + q * 128 : b * 256 + (q + 1) * 128
                 ]
     d = dot(wmb[...], v_buf[...])
+    second_a = across(first_a, sum_a, one_a, mine_a, two_a, s2a, r2a)
     for i in range(lonh):
         m = i // 2
         if i % 2 == 0:
@@ -328,16 +335,12 @@
         else:
             nxt = (m + 1) % (lonh // 2)
             grad = d[2 * C1 :, m * 128 : (m + 1) * 128] + d[:C1, nxt * 128 : (nxt + 1) * 128]
-        cot = grad.astype(BF16).astype(F32) * stem_slope[:, i * 128 : (i + 1) * 128]
+        cot = grad.astype(BF16).astype(F32) * slopes[:, i * 128 : (i + 1) * 128]
         cot = cot.astype(BF16)
         before = (i - 1) % lonh
         cc[0:C1, before * 128 : (before + 1) * 128] = cot
         cc[C1 : 2 * C1, i * 128 : (i + 1) * 128] = cot
         cot_send[i // per, :, (i % per) * 128 : (i % per + 1) * 128] = cot
-    second_a = across(first_a, sum_a, one_a, mine_a, two_a, s2a, r2a)
-    stem_sum = dot(e_buf[...], cc[...], ((1,), (1,)))
-    first_b = spread_out(stem_sum[:128], stem_sum[128:], sum_b, half_b, one_b, s1b, r1b)
-    third_a = gather(second_a, two_a, all_a, s3a, r3a)
     back = []
     for k in range(1, nl):
         to = lax.rem(me + k, nl)
@@ -346,6 +349,9 @@
         )
     own_back = pltpu.make_async_copy(cot_send.at[me], cot_out.at[me], own_sem.at[1])
     own_back.start()
+    stem_sum = dot(e_buf[...], cc[...], ((1,), (1,)))
+    first_b = spread_out(stem_sum[:128], stem_sum[128:], sum_b, half_b, one_b, s1b, r1b)
+    third_a = gather(second_a, two_a, all_a, s3a, r3a)
     for copy in moved + first_a:
         copy.wait_send()
     second_b = across(first_b, sum_b, one_b, mine_b, two_b, s2b, r2b)
@@ -438,6 +444,7 @@
             pltpu.VMEM((256, 384), BF16),
             pltpu.VMEM((128, 768), BF16),
             pltpu.VMEM((2 * C1, lonh * 128), F32),
+            pltpu.VMEM((C1, lonh * 128), F32),
             pltpu.VMEM((nl, C_IN * width, lat), BF16),
             pltpu.VMEM((256, lonh * 128), BF16),
             pltpu.VMEM((lonh // 2 * C1, 256), BF16),

time: 38.8 us -> 40.8 us (1.052)
  Pallas kernels: 38 us -> 40 us
    pallas_call x1, Pallas kernels: 35.9 us -> 37.8 us  [local(): pl.pallas_call(functools.partial(kernel, nl, nr), out_shape=[jax.ShapeDty...]
where the time goes in v4:
time: 40.8 us; the launch traced here: 40.6 us
  Pallas kernels  40 us (98%)
  between operations  0.64 us (2%)
    pallas_call x1, Pallas kernels, local(): pl.pallas_call(functools.partial(kernel, nl, nr), out_shape=[jax.ShapeDty...  37.8 us
    pallas_call x1, Pallas kernels, local(): pl.pallas_call(functools.partial(finish, 1.0 / (scen_here * nr)), out_sha...  2.14 us

profile of v4, /device:TPU:0, one launch (start us, length us, event | category | flops | bytes accessed | tf_op | source)
XLA Modules:
  0.0 40.6 jit_solution(3569454971508386181)
XLA Ops:
  0.6 37.8 %shard_map.109 = (f32[1,1024]{1,0:T(1,128)}, bf16[8,32,512]{2,1,0:T(8,128)(2,1)}, bf16[512,128]{1,0:T(8,128)(2,1)}, bf16[128,128]{1,0:T(8,128)(2,1)}) custom-call(bf16[8,192,256]{2,1,0:T(8,128)(2,1)} %bitcast.23, bf16[96,4,32]{2,1,0:T(4,128)(2,1)} %bitcast.25, bf16[288,64]{1,0:T(8,128)(2,1)} %bitcast.26, bf16[576,64]{1,0:T(8,128)(2,1)} %bitcast.24, ...), custom_call_target="tpu_custom_call" | custom-call | tf_op jit(solution)/shard_map/pallas_call | solution.py:426
  38.5 2.1 %shard_map.110 = (f32[16,64]{1,0:T(8,128)}, bf16[8,32,4,128]{3,2,1,0:T(4,128)(2,1)}, f32[96,4,32]{2,1,0:T(4,128)}, f32[288,64]{1,0:T(8,128)}, f32[576,64]{1,0:T(8,128)}, /*index=5*/f32[1,64]{1,0:T(1,128)}) custom-call(f32[1,1024]{1,0:T(1,128)} %get-tuple-element.16.pred, bf16[8,32,512]{2,1,0:T(8,128)(2,1)} %get-tuple-element.17.cot, ...), custom_call_target="tpu_custom_call" | custom-call | tf_op jit(solution)/shard_map/pallas_call | solution.py:474

commit v5 on v3

--- a/solution.py
+++ b/solution.py
@@ -62,7 +62,7 @@
 
 
 def sigmoid(v):
-    return 1.0 / (1.0 + jnp.exp(-v))
+    return 0.5 + 0.5 * jnp.tanh(0.5 * v)
 
 
 def slope_of(v, g):
@@ -96,7 +96,7 @@
     fields, ws_hbm, wm_hbm, wh_hbm, ow_hbm, pc_hbm,
     pred, cot_out, all_a, all_b,
     ws, wm, wh, ow_in, pc_in,
-    ws_all, wmb, pick_mid, spread_mid, y_buf,
+    ws_all, wmb, pick_mid, spread_mid,
     got, e_buf, a_rows, f_buf, v_buf, m_rows, col_r, cc, cot_send,
     sum_a, half_a, one_a, mine_a, two_a,
     sum_b, half_b, one_b, mine_b, two_b,
@@ -216,39 +216,35 @@
     spread_mid[...] = mid_spread()
     pick = stem_pick()
     order = slab_order(width)
-    group = per * 128
-
-    def stem_group(g):
-        where = pl.ds(pl.multiple_of(g * group, 128), group)
-        y_buf[:, where] = dot(ws_all[...], e_buf[:, where])
-
-    for k in range(nl):
-        if k == 0:
-            own.wait()
-            source = me
-        else:
-            moved[k - 1].wait_recv()
-            source = lax.rem(me - k + nl, nl)
-        lines = dot(order, got[source]).astype(BF16)
-        taps = dot(lines, pick).astype(BF16)
-        for l in range(width):
-            even = l % 2 == 0
-            tile = source * per + l // 2 - (1 if even else 0)
-            if l == 0:
-                tile = lax.rem(tile + lonh, lonh)
-            where = pl.ds(pl.multiple_of(tile * 128, 128), 128)
-            for b in range(4):
-                row = (128 if even else 0) + b * C_WIDE
-                e_buf[row : row + C_WIDE, where] = taps[
-                    l * C_WIDE : (l + 1) * C_WIDE, b * 128 : (b + 1) * 128
-                ]
-        if k > 0:
-            stem_group(source)
-    stem_group(me)
-
+
+    tall = width * C_WIDE
+    for batch in (range(0, 1), range(1, nl // 2), range(nl // 2, nl)):
+        for k in batch:
+            if k == 0:
+                own.wait()
+            else:
+                moved[k - 1].wait_recv()
+        sources = [lax.rem(me - k + nl, nl) for k in batch]
+        lines = [dot(order, got[source]).astype(BF16) for source in sources]
+        taps = dot(jnp.concatenate(lines, axis=0), pick).astype(BF16)
+        for at, source in enumerate(sources):
+            for l in range(width):
+                even = l % 2 == 0
+                tile = source * per + l // 2 - (1 if even else 0)
+                if l == 0:
+                    tile = lax.rem(tile + lonh, lonh)
+                where = pl.ds(pl.multiple_of(tile * 128, 128), 128)
+                top = at * tall + l * C_WIDE
+                for b in range(4):
+                    row = (128 if even else 0) + b * C_WIDE
+                    e_buf[row : row + C_WIDE, where] = taps[
+                        top : top + C_WIDE, b * 128 : (b + 1) * 128
+                    ]
+
+    both = dot(ws_all[...], e_buf[...])
     last = (lonh - 1) * 128
     stem_pre = (
-        jnp.concatenate([y_buf[0:C1, last:], y_buf[0:C1, :last]], axis=1) + y_buf[C1:, :]
+        jnp.concatenate([both[0:C1, last:], both[0:C1, :last]], axis=1) + both[C1:, :]
     )
     stem_g = sigmoid(stem_pre)
     stem_act = (stem_pre * stem_g).astype(BF16)
@@ -437,7 +433,6 @@
             pltpu.VMEM((96, 192), BF16),
             pltpu.VMEM((256, 384), BF16),
             pltpu.VMEM((128, 768), BF16),
-            pltpu.VMEM((2 * C1, lonh * 128), F32),
             pltpu.VMEM((nl, C_IN * width, lat), BF16),
             pltpu.VMEM((256, lonh * 128), BF16),
             pltpu.VMEM((lonh // 2 * C1, 256), BF16),

time: 38.8 us -> 38.1 us (0.982)
  Pallas kernels: 38 us -> 37.4 us
    pallas_call x1, Pallas kernels: 35.9 us -> 35.2 us  [local(): pl.pallas_call(functools.partial(kernel, nl, nr), out_shape=[jax.ShapeDty...]
where the time goes in v5:
time: 38.1 us; the launch traced here: 38 us
  Pallas kernels  37.4 us (98%)
  between operations  0.64 us (2%)
    pallas_call x1, Pallas kernels, local(): pl.pallas_call(functools.partial(kernel, nl, nr), out_shape=[jax.ShapeDty...  35.2 us
    pallas_call x1, Pallas kernels, local(): pl.pallas_call(functools.partial(finish, 1.0 / (scen_here * nr)), out_sha...  2.14 us

profile of v5, /device:TPU:0, one launch (start us, length us, event | category | flops | bytes accessed | tf_op | source)
XLA Modules:
  0.0 38.0 jit_solution(4967045262523334915)
XLA Ops:
  0.6 35.2 %shard_map.109 = (f32[1,1024]{1,0:T(1,128)}, bf16[8,32,512]{2,1,0:T(8,128)(2,1)}, bf16[512,128]{1,0:T(8,128)(2,1)}, bf16[128,128]{1,0:T(8,128)(2,1)}) custom-call(bf16[8,192,256]{2,1,0:T(8,128)(2,1)} %bitcast.23, bf16[96,4,32]{2,1,0:T(4,128)(2,1)} %bitcast.25, bf16[288,64]{1,0:T(8,128)(2,1)} %bitcast.26, bf16[576,64]{1,0:T(8,128)(2,1)} %bitcast.24, ...), custom_call_target="tpu_custom_call" | custom-call | tf_op jit(solution)/shard_map/pallas_call | solution.py:416
  35.9 2.1 %shard_map.110 = (f32[16,64]{1,0:T(8,128)}, bf16[8,32,4,128]{3,2,1,0:T(4,128)(2,1)}, f32[96,4,32]{2,1,0:T(4,128)}, f32[288,64]{1,0:T(8,128)}, f32[576,64]{1,0:T(8,128)}, /*index=5*/f32[1,64]{1,0:T(1,128)}) custom-call(f32[1,1024]{1,0:T(1,128)} %get-tuple-element.16.pred, bf16[8,32,512]{2,1,0:T(8,128)(2,1)} %get-tuple-element.17.cot, ...), custom_call_target="tpu_custom_call" | custom-call | tf_op jit(solution)/shard_map/pallas_call | solution.py:462
